TPU v7x, 768 devices: a whole 4x8x12 slice. The times are simulated.
768 devices in a mesh: dp: 64 (over x, y, core), group: 12 (over z).
Axes of the slice: x: 4, y: 8, z: 12, core: 2. Of those that a mesh axis runs over, the one named last changes fastest.
Arguments:
- grad: float32 [12, 9216, 128], P('group', 'dp'), may hold values from -6000 to 6000
- momentum: float32 [12, 9216, 128], P('group', 'dp'), may hold values from -6 to 6
Outputs:
- momentum_out: float32 [12, 9216, 128], P('group', 'dp')
- update: bfloat16 [12, 9216, 128], P('group', 'dp')
All inputs are finite; a program needn't handle non-finite values.
Results may differ from a plain program's by a relative error of at most 0.002.
The roundings to bfloat16 on the way count: a program that leaves them out, or rounds other values in their place, can miss the bound.
Values may be sent and summed in bfloat16 or wider, within the bound.
No kernel may reach another device: no remote copies, remote signals or barrier semaphores. Data moves between devices by JAX's collectives and lax.ppermute only.
A program may use at most 32 MiB of HBM per device.

v0:
```python
import math

import jax
import jax.numpy as jnp
from jax import lax
from jax.sharding import PartitionSpec as P

ROWS = 576
ITERS = 2


momentum_rate = 0.95
target_rms = 0.5
coef_first = 3.4445
coef_second = -4.775
coef_third = 2.0315


def self_gram(iterate):
    return jnp.einsum("lcr,lcs->lrs", iterate, iterate, preferred_element_type=jnp.float32)


def poly_from_gram(gram_matrix):
    gram_low = gram_matrix.astype(jnp.bfloat16)
    squared = jnp.einsum("lrs,lst->lrt", gram_low, gram_low, preferred_element_type=jnp.float32)
    return (coef_second * gram_matrix + coef_third * squared).astype(jnp.bfloat16)


def apply_poly(iterate, polynomial):
    product = jnp.einsum("lcr,lrs->lcs", iterate, polynomial, preferred_element_type=jnp.float32)
    return coef_first * iterate.astype(jnp.float32) + product


def local(grad, momentum):
    layers_here = grad.shape[0]
    flat_rows = grad.shape[1]
    devices_dp = lax.axis_size("dp")
    groups = lax.axis_size("group")
    local_cols = flat_rows * 128 // ROWS
    entries = layers_here * groups * ROWS * local_cols * devices_dp
    update_scale = 0.2 * math.sqrt(max(ROWS, local_cols * devices_dp))
    square = lax.psum(jnp.sum(grad * grad), ("dp", "group"))
    grad_scale = target_rms / (jnp.sqrt(square / entries) + 1e-06)
    momentum_out = momentum_rate * momentum + grad_scale * grad
    nudged = grad_scale * grad + momentum_rate * momentum_out
    unorm_square = lax.psum(jnp.sum(nudged * nudged, axis=(1, 2)), "dp")
    scaled = nudged / (jnp.sqrt(unorm_square)[:, None, None] + 1e-07)
    iterate = scaled.astype(jnp.bfloat16).reshape(layers_here, local_cols, ROWS)
    combined = None
    for step in range(ITERS):
        gram_matrix = lax.psum(self_gram(iterate), "dp")
        combined = apply_poly(iterate, poly_from_gram(gram_matrix))
        if step + 1 < ITERS:
            iterate = combined.astype(jnp.bfloat16)
    update = (update_scale * combined).astype(jnp.bfloat16)
    return (momentum_out, update.reshape(layers_here, flat_rows, 128))


def solution(mesh):
    return jax.shard_map(
        local,
        mesh=mesh,
        in_specs=(P("group", "dp", None), P("group", "dp", None)),
        out_specs=(P("group", "dp", None), P("group", "dp", None)),
        check_vma=False,
    )
```

profile of v0, /device:TPU:1, one launch (start us, length us, event | category | flops | bytes accessed | tf_op | source)
XLA Modules:
  0.0 678.9 jit_solution(17289019088310587793)
XLA Ops:
  7.2 0.0 all-reduce.3.cloned.1.call-start
  7.2 1.5 multiply_reduce_fusion.1
  8.7 120.5 %psum.28 = f32[]{:T(128)} all-reduce(f32[]{:T(128)} %multiply_reduce_fusion.1), channel_id=1, replica_groups=mesh['dp'=64,'group'=12] {'dp','group'}, use_global_device_ids=true, to_apply=%region_1.0 | all-reduce | flops 1 | bytes 8 | tf_op jit(solution)/shard_map/psum | solution.py:42
  129.9 1.5 multiply_reduce_fusion
  131.5 0.0 copy-start
  131.5 124.7 %psum.29 = f32[1]{0:T(128)} all-reduce(f32[1]{0:T(128)} %bitcast), channel_id=1, replica_groups=mesh['dp'=64,'group'=12] {'dp'}, use_global_device_ids=true, to_apply=%region_3.0 | all-reduce | flops 1 | bytes 8 | tf_op jit(solution)/shard_map/psum | solution.py:46
  256.9 0.9 divide_convert_fusion
  257.8 0.1 reshape.61
  257.9 1.5 convolution_bitcast_fusion.1
  259.4 0.0 all-reduce.3.cloned.1.call-update
  259.4 0.0 copy-done
  259.4 0.0 all-reduce.5.cloned.1.call-start
  259.5 195.7 %all-reduce.3.cloned.1.call-done = f32[1,576,576]{2,1,0:T(8,128)} async-done(((f32[1,576,576]{2,1,0:T(8,128)}), f32[1,576,576]{2,1,0:T(8,128)}) %all-reduce.3.cloned.1.call-update) | async-done | bytes 1327120 | tf_op jit(solution)/shard_map/psum | solution.py:51
  455.1 3.6 fusion.5
  458.7 1.5 convolution_bitcast_fusion
  460.2 0.0 all-reduce.5.cloned.1.call-update
  460.2 207.5 %all-reduce.5.cloned.1.call-done = f32[1,576,576]{2,1,0:T(8,128)} async-done(((f32[1,576,576]{2,1,0:T(8,128)}), f32[1,576,576]{2,1,0:T(8,128)}) %all-reduce.5.cloned.1.call-update) | async-done | bytes 1327120 | tf_op jit(solution)/shard_map/psum | solution.py:51
  667.7 3.6 fusion.6
  671.3 0.7 reshape.66
Async XLA Ops:
  7.2 448.0 %all-reduce.3.cloned.1.call-start = ((), (), s32[]{:S(2)}) async-start(), calls=%async_computation | async-start | bytes 2949120 | tf_op jit(solution)/shard_map/psum | solution.py:51
  131.5 127.9 %copy-start = (f32[1,144,128]{2,1,0:T(8,128)}, f32[1,144,128]{2,1,0:T(8,128)S(1)}, u32[]{:S(2)}) copy-start(f32[1,144,128]{2,1,0:T(8,128)S(1)} %get-tuple-element.3) | copy-start | bytes 221188
  259.4 408.3 %all-reduce.5.cloned.1.call-start = ((), (), s32[]{:S(2)}) async-start(), calls=%async_computation.1 | async-start | bytes 2949120 | tf_op jit(solution)/shard_map/psum | solution.py:51
Sparse Core Ops, SparseCore 0:
  259.5 195.5 all-reduce.2
  460.4 207.3 all-reduce.4
where the time goes:
time: 681 us; the launch traced here: 679 us
  waiting for transfers between devices  403 us (59%)
  blocking collectives  245 us (36%)
  between operations  15.5 us (2%)
  matrix products  10.1 us (1%)
    psum x2, waiting for transfers between devices, local(): gram_matrix = lax.psum(self_gram(iterate), 'dp')  403 us
    psum x1, blocking collectives, local(): unorm_square = lax.psum(jnp.sum(nudged * nudged, axis=(1, 2)), 'dp')  125 us
    psum x1, blocking collectives, local(): square = lax.psum(jnp.sum(grad * grad), ('dp', 'group'))  120 us
  transfers between devices with their start and end apart: 2, of which 2 were waited for; matrix products, arithmetic and copies ran while one was open for 0% of the time, Pallas kernels for 0%

commit v1 on v0

v1 whole, which is shorter than its diff:
```python
import functools
import math

import jax
import jax.numpy as jnp
import numpy as np
from jax import lax
from jax.experimental import pallas as pl
from jax.experimental.pallas import tpu as pltpu
from jax.sharding import Mesh, PartitionSpec as P

ROWS = 576
ITERS = 2

momentum_rate = 0.95
target_rms = 0.5
coef_first = 3.4445
coef_second = -4.775
coef_third = 2.0315

f32, bf16 = jnp.float32, jnp.bfloat16
VMEM = pl.BlockSpec(memory_space=pltpu.VMEM)
SMEM = pl.BlockSpec(memory_space=pltpu.SMEM)
NT = (((1,), (1,)), ((), ()))


def two_sum(a, b):
    s = a + b
    t = s - a
    return s, (a - (s - t)) + (b - t)


def fast_two_sum(a, b):
    s = a + b
    return s, b - (s - a)


def split(a):
    t = 4097.0 * a
    high = t - (t - a)
    return high, a - high


def two_prod(a, b):
    p = a * b
    ah, al = split(a)
    bh, bl = split(b)
    return p, ((ah * bh - p) + ah * bl + al * bh) + al * bl


def dd_add(a, b):
    s, e = two_sum(a[0], b[0])
    return fast_two_sum(s, e + (a[1] + b[1]))


def dd_mul(a, b):
    p, e = two_prod(a[0], b[0])
    return fast_two_sum(p, e + (a[0] * b[1] + a[1] * b[0]))


def dd_const(value):
    high = np.float32(value)
    return float(high), float(np.float32(value - float(high)))


def tile_tree(values):
    while len(values) > 1:
        paired = [dd_add(values[i], values[i + 1]) for i in range(0, len(values) - 1, 2)]
        values = paired + ([values[-1]] if len(values) % 2 else [])
    return values[0]


def all_lanes(a):
    for axis, shifts in ((0, (4, 2, 1)), (1, (64, 32, 16, 8, 4, 2, 1))):
        for shift in shifts:
            a = dd_add(a, (pltpu.roll(a[0], shift, axis), pltpu.roll(a[1], shift, axis)))
    return a


def pack_rows(values):
    row = lax.broadcasted_iota(jnp.int32, (8, 128), 0)
    tile = jnp.zeros((8, 128), f32)
    for i, (high, low) in enumerate(values):
        tile = jnp.where(row == i, high, jnp.where(row == i + 4, low, tile))
    return tile


def unpack(tile):
    return tile, pltpu.roll(tile, 4, 0)


def repack(pair):
    row = lax.broadcasted_iota(jnp.int32, (8, 128), 0)
    return jnp.where(row < 4, pair[0], pltpu.roll(pair[1], 4, 0))


def sums_kernel(copies, grad_ref, momentum_ref, out_ref):
    rows = grad_ref.shape[1]
    gg, gm, mm = [], [], []
    for i in range(0, rows, 8):
        g = grad_ref[0, i : i + 8, :]
        m = momentum_ref[0, i : i + 8, :]
        gg.append(two_prod(g, g))
        gm.append(two_prod(g, m))
        mm.append(two_prod(m, m))
    tile = pack_rows([all_lanes(tile_tree(v)) for v in (gg, gm, mm)])
    for i in range(copies):
        out_ref[i] = tile


def combine_kernel(copies, in_ref, out_ref):
    tile = repack(tile_tree([unpack(in_ref[i]) for i in range(in_ref.shape[0])]))
    for i in range(copies):
        out_ref[i] = tile


def scale_kernel(entries, groups, copies, group_ref, in_ref, grad_ref, momentum_ref, momentum_out_ref, out_ref):
    group = group_ref[0]
    whole = tile_tree([unpack(in_ref[i]) for i in range(in_ref.shape[0])])
    own = tile_tree([unpack(in_ref[group + i]) for i in range(0, in_ref.shape[0], groups)])
    square = whole[0][0:1]
    grad_scale = target_rms / (jnp.sqrt(square / entries) + 1e-06)
    rate = float(np.float32(momentum_rate))
    gg = (own[0][0:1], own[1][0:1])
    gm = (own[0][1:2], own[1][1:2])
    mm = (own[0][2:3], own[1][2:3])
    factor_high, factor_low = dd_const(1.0 + rate)
    ones = jnp.ones_like(grad_scale)
    a = two_prod(grad_scale, factor_high * ones)
    a = fast_two_sum(a[0], a[1] + grad_scale * factor_low)
    b = tuple(v * ones for v in dd_const(rate * rate))
    ag = dd_mul(a, gg)
    cross = dd_mul(dd_mul((2.0 * a[0], 2.0 * a[1]), b), gm)
    total = dd_add(dd_add(dd_mul(a, ag), dd_mul(dd_mul(b, b), mm)), cross)
    unorm = jnp.sqrt(jnp.maximum(total[0], 0.0))
    scaled_grad = grad_scale * grad_ref[0]
    momentum_out = momentum_rate * momentum_ref[0] + scaled_grad
    nudged = scaled_grad + momentum_rate * momentum_out
    momentum_out_ref[0] = momentum_out
    iterate = (nudged / (unorm + 1e-07)).astype(bf16)
    for i in range(copies):
        out_ref[i] = iterate


def transpose_kernel(copies, in_ref, out_ref, flat_ref):
    blocks, rows = in_ref.shape[:2]
    for i in range(blocks):
        flat_ref[i * rows : (i + 1) * rows, :] = in_ref[i].astype(f32)
    half = blocks * rows // 9
    for j in range(9):
        turned = flat_ref[pl.ds(j, half, stride=9), :].T.astype(bf16)
        for i in range(copies):
            if j < 4:
                out_ref[i, 128 * j : 128 * j + 128, 0:half] = turned
            elif j == 4:
                out_ref[i, 512:576, 0:half] = turned[0:64]
                out_ref[i, 0:64, half : 2 * half] = turned[64:128]
            else:
                out_ref[i, 128 * j - 576 : 128 * j - 448, half : 2 * half] = turned


def own_load(flat_ref, pairs):
    low = lax.broadcasted_iota(jnp.int32, (pairs, 128), 1) < 64
    flat = [flat_ref[pl.ds(j, pairs, stride=9), :] for j in range(9)]
    turned = [pltpu.roll(flat[j], 64, 1) for j in range(4, 9)]
    even = flat[:4] + [flat[4]]
    odd = [jnp.where(low, turned[k], turned[k + 1]) for k in range(4)] + [turned[4]]
    return jnp.concatenate([jnp.concatenate(even, 1), jnp.concatenate(odd, 1)], 0)[:, :ROWS]


def own_store(flat_ref, value, pairs):
    value = jnp.concatenate([value, jnp.zeros((2 * pairs, 64), f32)], 1)
    low = lax.broadcasted_iota(jnp.int32, (pairs, 128), 1) < 64
    even = [value[:pairs, 128 * j : 128 * j + 128] for j in range(5)]
    odd = [pltpu.roll(value[pairs:, 128 * j : 128 * j + 128], 64, 1) for j in range(5)]
    flat = even[:4] + [jnp.where(low, even[4], odd[0])]
    flat += [jnp.where(low, odd[k], odd[k + 1]) for k in range(4)]
    for j in range(9):
        flat_ref[pl.ds(j, pairs, stride=9), :] = flat[j]


def iterate_kernel(update_scale, mine_ref, other_ref, own_ref, out_ref, poly_ref, next_ref, flat_ref):
    blocks = [(r, i) for r in (mine_ref, other_ref) for i in range(r.shape[0])]
    pairs = own_ref.shape[0] // 9

    def gram(get):
        total = None
        for i in range(len(blocks)):
            v = get(i)
            d = lax.dot_general(v, v, NT, preferred_element_type=f32)
            total = d if total is None else total + d
        return total

    def poly(gram_matrix):
        low = gram_matrix.astype(bf16)
        squared = jnp.dot(low, low, preferred_element_type=f32)
        return (coef_second * gram_matrix + coef_third * squared).astype(bf16)

    poly_ref[...] = poly(gram(lambda i: blocks[i][0][blocks[i][1]]))
    for i, (r, k) in enumerate(blocks):
        v = r[k]
        product = jnp.dot(poly_ref[...], v, preferred_element_type=f32)
        next_ref[i] = (coef_first * v.astype(f32) + product).astype(bf16)
    flat_ref[...] = own_ref[...].astype(f32)
    own = own_load(flat_ref, pairs)
    product = jnp.dot(own.astype(bf16), poly_ref[...], preferred_element_type=f32)
    own = (coef_first * own + product).astype(bf16)
    poly_ref[...] = poly(gram(lambda i: next_ref[i]))
    product = jnp.dot(own, poly_ref[...], preferred_element_type=f32)
    own_store(flat_ref, update_scale * (coef_first * own.astype(f32) + product), pairs)
    out_ref[0] = flat_ref[...].astype(bf16)


def kernel(body, name, out, n_in, scratch=(), in_specs=None):
    return pl.pallas_call(
        body,
        name=name,
        out_shape=out,
        in_specs=in_specs or [VMEM] * n_in,
        out_specs=jax.tree.map(lambda _: VMEM, out),
        scratch_shapes=list(scratch),
        compiler_params=pltpu.CompilerParams(vmem_limit_bytes=48 * 2**20),
    )


def local(entries, update_scale, sizes, grad, momentum):
    nx, ny, nc, ng = sizes
    rows = grad.shape[1]
    shape = jax.ShapeDtypeStruct
    sums = kernel(functools.partial(sums_kernel, nx * ny), "sums", shape((nx * ny, 8, 128), f32), 2)(grad, momentum)
    sums = lax.all_to_all(sums, ("x", "y"), 0, 0)
    sums = kernel(functools.partial(combine_kernel, nc * ng), "combine", shape((nc * ng, 8, 128), f32), 1)(sums)
    sums = lax.all_to_all(sums, ("core", "group"), 0, 0)
    group = lax.axis_index("group").astype(jnp.int32).reshape(1)
    momentum_out, iterate = kernel(
        functools.partial(scale_kernel, entries, ng, ny),
        "scale",
        (shape(grad.shape, f32), shape((ny, rows, 128), bf16)),
        4,
        in_specs=[SMEM, VMEM, VMEM, VMEM],
    )(group, sums, grad, momentum)
    own = iterate[0]
    gathered = lax.all_to_all(iterate, "y", 0, 0)
    columns = ny * rows * 128 // ROWS
    turned = kernel(
        functools.partial(transpose_kernel, nx),
        "turn",
        shape((nx, ROWS, columns), bf16),
        1,
        scratch=[pltpu.VMEM((ny * rows, 128), f32)],
    )(gathered)
    mine = lax.all_to_all(turned, "x", 0, 0)
    other = lax.ppermute(mine, "core", [(0, 1), (1, 0)])
    update = kernel(
        functools.partial(iterate_kernel, update_scale),
        "newton",
        shape(grad.shape, bf16),
        3,
        scratch=[
            pltpu.VMEM((ROWS, ROWS), bf16),
            pltpu.VMEM((2 * nx, ROWS, columns), bf16),
            pltpu.VMEM((rows, 128), f32),
        ],
    )(mine, other, own)
    return momentum_out, update


def solution(mesh):
    sizes = (4, 8, 2, 12)
    split_mesh = Mesh(mesh.devices.reshape(sizes), ("x", "y", "core", "group"))
    spec = P("group", ("x", "y", "core"), None)

    def run(grad, momentum):
        entries = grad.size
        layers, flat_rows, _ = grad.shape
        width = flat_rows * 128 // ROWS
        update_scale = 0.2 * math.sqrt(max(ROWS, width))
        return jax.shard_map(
            functools.partial(local, entries, update_scale, sizes),
            mesh=split_mesh,
            in_specs=(spec, spec),
            out_specs=(spec, spec),
            check_vma=False,
        )(grad, momentum)

    return run
```

time: 681 us -> 102 us (0.15)
  waiting for transfers between devices: 403 us -> 13.1 us
  blocking collectives: 245 us -> 48 us
  starting transfers between devices: 0.08 us -> 23.3 us
  between operations: 15.5 us -> 0.69 us
  Pallas kernels: 0 us -> 12.7 us
  matrix products: 10.1 us -> 0 us
    psum x2 -> x0, waiting for transfers between devices: 403 us -> none  [local(): gram_matrix = lax.psum(self_gram(iterate), 'dp')]
    psum x2 -> x0, blocking collectives: 245 us -> none  [the longest x1 125 us: local(): unorm_square = lax.psum(jnp.sum(nudged * nudged, axis=(1, 2)), 'dp')]
    all_to_all x0 -> x3, blocking collectives: none -> 48 us  [the longest x1 19.4 us: local(): sums = lax.all_to_all(sums, ('x', 'y'), 0, 0)]
    all_to_all x0 -> x1, starting transfers between devices: none -> 17.3 us  [local(): sums = lax.all_to_all(sums, ('core', 'group'), 0, 0)]
    pallas_call x0 -> x5, Pallas kernels: none -> 12.7 us  [the longest x1 10.3 us: local(): kernel(functools.partial(iterate_kernel, update_scale), 'newton', shape(g...]
    all_to_all x0 -> x1, waiting for transfers between devices: none -> 10.7 us  [local(): sums = lax.all_to_all(sums, ('core', 'group'), 0, 0)]
    dot_general x4 -> x0, matrix products: 10.1 us -> none  [the longest x2 7.13 us: apply_poly(): jnp.einsum('lcr,lrs->lcs', iterate, polynomial, preferred_element_type=jn...]
where the time goes in v1:
time: 102 us; the launch traced here: 101 us
  blocking collectives  48 us (47%)
  starting transfers between devices  23.3 us (23%)
  waiting for transfers between devices  13.1 us (13%)
  Pallas kernels  12.7 us (12%)
  local copies, waits for them, and re-layouts  3.54 us (3%)
    all_to_all x1, blocking collectives, local(): sums = lax.all_to_all(sums, ('x', 'y'), 0, 0)  19.4 us
    all_to_all x1, starting transfers between devices, local(): sums = lax.all_to_all(sums, ('core', 'group'), 0, 0)  17.3 us
    all_to_all x1, blocking collectives, local(): mine = lax.all_to_all(turned, 'x', 0, 0)  15.8 us
    all_to_all x1, blocking collectives, local(): gathered = lax.all_to_all(iterate, 'y', 0, 0)  12.8 us
    all_to_all x1, waiting for transfers between devices, local(): sums = lax.all_to_all(sums, ('core', 'group'), 0, 0)  10.7 us
    pallas_call x1, Pallas kernels, local(): kernel(functools.partial(iterate_kernel, update_scale), 'newton', shape(g...  10.3 us
    ppermute x1, starting transfers between devices, local(): other = lax.ppermute(mine, 'core', [(0, 1), (1, 0)])  6.02 us
    unnamed x8, local copies, waits for them, and re-layouts  3.53 us
  transfers between devices with their start and end apart: 2, of which 2 were waited for; matrix products, arithmetic and copies ran while one was open for 0% of the time, Pallas kernels for 0%

profile of v1, /device:TPU:1, one launch (start us, length us, event | category | flops | bytes accessed | tf_op | source)
XLA Modules:
  0.0 101.3 jit_solution(14754690220398125711)
XLA Ops:
  0.6 0.0 copy-start
  0.6 0.9 copy-done
  1.5 0.0 copy-start.2
  1.5 0.9 copy-done.2
  2.4 0.7 sums.1
  3.1 19.4 %all_to_all.20.in_ref = f32[32,8,128]{2,1,0:T(8,128)S(1)} all-to-all(f32[32,8,128]{2,1,0:T(8,128)S(1)} %sums.1), channel_id=1, replica_groups=mesh['x'=4,'y'=8,'core'=2,'group'=12] {'x','y'}, dimensions={0} | all-to-all | bytes 262144 | tf_op jit(solution)/shard_map/all_to_all | solution.py:231
  22.6 0.7 combine.1
  23.3 17.3 %all-to-all-start.1 = ((f32[24,8,128]{2,1,0:T(8,128)}), f32[24,8,128]{2,1,0:T(8,128)S(1)}, u32[]{:S(2)}, u32[]{:S(2)}) async-start(f32[24,8,128]{2,1,0:T(8,128)} %combine.1), calls=%async_computation.1 | async-start | bytes 196608 | tf_op jit(solution)/shard_map/all_to_all | solution.py:233
  40.6 10.7 %all-to-all-done.1.in_ref = f32[24,8,128]{2,1,0:T(8,128)S(1)} async-done(((f32[24,8,128]{2,1,0:T(8,128)}), f32[24,8,128]{2,1,0:T(8,128)S(1)}, u32[]{:S(2)}, u32[]{:S(2)}) %all-to-all-start.1) | async-done | bytes 98336 | tf_op jit(solution)/shard_map/all_to_all | solution.py:233
  51.3 0.0 copy-start.1
  51.3 0.9 copy-done.1
  52.2 0.0 copy-start.3
  52.2 0.9 copy-done.3
  53.1 0.7 scale.1
  53.8 12.8 %all_to_all.21.in_ref = bf16[8,144,128]{2,1,0:T(8,128)(2,1)S(1)} all-to-all(bf16[8,144,128]{2,1,0:T(8,128)(2,1)S(1)} %get-tuple-element.5), channel_id=1, replica_groups=mesh['x'=4,'y'=8,'core'=2,'group'=12] {'y'}, dimensions={0} | all-to-all | bytes 589824 | tf_op jit(solution)/shard_map/all_to_all | solution.py:243
  66.6 0.3 turn.1
  66.8 15.8 %all_to_all.22.mine_ref = bf16[4,576,256]{2,1,0:T(8,128)(2,1)S(1)} all-to-all(bf16[4,576,256]{2,1,0:T(8,128)(2,1)S(1)} %turn.1), channel_id=1, replica_groups=mesh['x'=4,'y'=8,'core'=2,'group'=12] {'x'}, dimensions={0} | all-to-all | bytes 2359296 | tf_op jit(solution)/shard_map/all_to_all | solution.py:252
  82.6 6.0 %collective-permute-start = (bf16[4,576,256]{2,1,0:T(8,128)(2,1)S(1)}, bf16[4,576,256]{2,1,0:T(8,128)(2,1)S(1)}, u32[]{:S(2)}, u32[]{:S(2)}) collective-permute-start(bf16[4,576,256]{2,1,0:T(8,128)(2,1)S(1)} %all_to_all.22.mine_ref), channel_id=1, source_target_pairs={{0,12},{12,0},{1,13},{13,1},{2,14},{14,2},{3,15},{15,3},{4,16},{16... | collective-permute-start | bytes 3538952 | tf_op jit(solution)/shard_map/ppermute | solution.py:253
  88.6 2.4 %collective-permute-done.other_ref = bf16[4,576,256]{2,1,0:T(8,128)(2,1)S(1)} collective-permute-done((bf16[4,576,256]{2,1,0:T(8,128)(2,1)S(1)}, bf16[4,576,256]{2,1,0:T(8,128)(2,1)S(1)}, u32[]{:S(2)}, u32[]{:S(2)}) %collective-permute-start) | collective-permute-done | bytes 1179680 | tf_op jit(solution)/shard_map/ppermute | solution.py:253
  91.1 10.3 %newton.1 = bf16[1,144,128]{2,1,0:T(8,128)(2,1)} custom-call(bf16[4,576,256]{2,1,0:T(8,128)(2,1)S(1)} %all_to_all.22.mine_ref, bf16[4,576,256]{2,1,0:T(8,128)(2,1)S(1)} %collective-permute-done.other_ref, bf16[144,128]{1,0:T(8,128)(2,1)S(1)} %slice_bitcast_fusion.own_ref), custom_call_target="tpu_custom_call" | custom-call | tf_op jit(solution)/shard_map/newton/pallas_call | solution.py:254
  (1 shorter events, 0.0 us)
Async XLA Ops:
  0.6 0.9 copy-start
  1.5 0.9 copy-start.2
  23.3 28.0 %all-to-all-start.1 = ((f32[24,8,128]{2,1,0:T(8,128)}), f32[24,8,128]{2,1,0:T(8,128)S(1)}, u32[]{:S(2)}, u32[]{:S(2)}) async-start(f32[24,8,128]{2,1,0:T(8,128)} %combine.1), calls=%async_computation.1 | async-start | bytes 196608 | tf_op jit(solution)/shard_map/all_to_all | solution.py:233
  51.3 0.9 copy-start.1
  52.2 0.9 copy-start.3
  82.6 8.5 %collective-permute-start = (bf16[4,576,256]{2,1,0:T(8,128)(2,1)S(1)}, bf16[4,576,256]{2,1,0:T(8,128)(2,1)S(1)}, u32[]{:S(2)}, u32[]{:S(2)}) collective-permute-start(bf16[4,576,256]{2,1,0:T(8,128)(2,1)S(1)} %all_to_all.22.mine_ref), channel_id=1, source_target_pairs={{0,12},{12,0},{1,13},{13,1},{2,14},{14,2},{3,15},{15,3},{4,16},{16... | collective-permute-start | bytes 3538952 | tf_op jit(solution)/shard_map/ppermute | solution.py:253

commit v2 on v1

v2 whole, which is shorter than its diff:
```python
import functools
import math

import jax
import jax.numpy as jnp
import numpy as np
from jax import lax
from jax.experimental import pallas as pl
from jax.experimental.pallas import tpu as pltpu
from jax.sharding import Mesh, PartitionSpec as P

ROWS = 576
ITERS = 2

momentum_rate = 0.95
target_rms = 0.5
coef_first = 3.4445
coef_second = -4.775
coef_third = 2.0315

f32, bf16 = jnp.float32, jnp.bfloat16
VMEM = pl.BlockSpec(memory_space=pltpu.VMEM)
SMEM = pl.BlockSpec(memory_space=pltpu.SMEM)
NT = (((1,), (1,)), ((), ()))


def two_sum(a, b):
    s = a + b
    t = s - a
    return s, (a - (s - t)) + (b - t)


def fast_two_sum(a, b):
    s = a + b
    return s, b - (s - a)


def split(a):
    t = 4097.0 * a
    high = t - (t - a)
    return high, a - high


def two_prod(a, b):
    p = a * b
    ah, al = split(a)
    bh, bl = split(b)
    return p, ((ah * bh - p) + ah * bl + al * bh) + al * bl


def dd_add(a, b):
    s, e = two_sum(a[0], b[0])
    return fast_two_sum(s, e + (a[1] + b[1]))


def dd_mul(a, b):
    p, e = two_prod(a[0], b[0])
    return fast_two_sum(p, e + (a[0] * b[1] + a[1] * b[0]))


def dd_const(value):
    high = np.float32(value)
    return float(high), float(np.float32(value - float(high)))


def tree(values):
    while len(values) > 1:
        paired = [dd_add(values[i], values[i + 1]) for i in range(0, len(values) - 1, 2)]
        values = paired + ([values[-1]] if len(values) % 2 else [])
    return values[0]


def fold(a, axis, shifts):
    for shift in shifts:
        a = dd_add(a, (pltpu.roll(a[0], shift, axis), pltpu.roll(a[1], shift, axis)))
    return a


def lanes():
    return lax.broadcasted_iota(jnp.int32, (8, 128), 1)


def pack(values):
    lane = lanes()
    tile = jnp.zeros((8, 128), f32)
    for i, (high, low) in enumerate(values):
        tile = jnp.where(lane == i, high, jnp.where(lane == i + 64, low, tile))
    return tile


def add_rows(ref):
    zero = jnp.zeros((8, 128), f32)
    high, low = fold(tree([(ref[i : i + 8, :], zero) for i in range(0, ref.shape[0], 8)]), 0, (4, 2, 1))
    return fast_two_sum(high, low + pltpu.roll(high, 64, 1))


def sums_kernel(grad_ref, momentum_ref, out_ref, grad_out_ref, momentum_out_ref):
    grad_out_ref[...] = grad_ref[...]
    momentum_out_ref[...] = momentum_ref[...]
    gg, gm, mm = [], [], []
    for i in range(0, grad_ref.shape[1], 8):
        g = grad_ref[0, i : i + 8, :]
        m = momentum_ref[0, i : i + 8, :]
        gg.append(two_prod(g, g))
        gm.append(two_prod(g, m))
        mm.append(two_prod(m, m))
    sums = [fold(fold(tree(v), 0, (4, 2, 1)), 1, (64, 32, 16, 8, 4, 2, 1)) for v in (gg, gm, mm)]
    tile = pack([sums[0]] + sums)
    for i in range(0, out_ref.shape[0], 8):
        out_ref[i : i + 8, :] = tile


def combine_kernel(groups, group_ref, in_ref, out_ref):
    high, low = add_rows(in_ref)
    lane = lanes()
    tile = jnp.where(lane < 64, high, pltpu.roll(low, 64, 1))
    for i in range(0, out_ref.shape[0], 8):
        to = lax.rem(lax.broadcasted_iota(jnp.int32, (8, 128), 0) + i, groups)
        keep = (to == group_ref[0]) | (lax.rem(lane, 64) == 0)
        out_ref[i : i + 8, :] = jnp.where(keep, tile, 0.0)


def scale_kernel(entries, in_ref, grad_ref, momentum_ref, out_ref, own_ref, scale_ref):
    high, low = add_rows(in_ref)
    lane = lanes()

    def value(i):
        return tuple(jnp.sum(jnp.where(lane == i, v, 0.0), axis=1, keepdims=True)[0:1] for v in (high, low))

    square, gg, gm, mm = (value(i) for i in range(4))
    grad_scale = target_rms / (jnp.sqrt(square[0] / entries) + 1e-06)
    rate = float(np.float32(momentum_rate))
    factor_high, factor_low = dd_const(1.0 + rate)
    ones = jnp.ones_like(grad_scale)
    a = two_prod(grad_scale, factor_high * ones)
    a = fast_two_sum(a[0], a[1] + grad_scale * factor_low)
    b = tuple(v * ones for v in dd_const(rate * rate))
    cross = dd_mul(dd_mul((2.0 * a[0], 2.0 * a[1]), b), gm)
    total = dd_add(dd_add(dd_mul(a, dd_mul(a, gg)), dd_mul(dd_mul(b, b), mm)), cross)
    unorm = jnp.sqrt(jnp.maximum(total[0], 0.0))
    scaled_grad = grad_scale * grad_ref[0]
    nudged = scaled_grad + momentum_rate * (momentum_rate * momentum_ref[0] + scaled_grad)
    iterate = (nudged / (unorm + 1e-07)).astype(bf16)
    for i in range(out_ref.shape[0]):
        out_ref[i] = iterate
    own_ref[...] = iterate.astype(f32)
    scale_ref[...] = jnp.broadcast_to(grad_scale, scale_ref.shape)


def transpose_kernel(copies, in_ref, out_ref, flat_ref):
    blocks, rows = in_ref.shape[:2]
    for i in range(blocks):
        flat_ref[i * rows : (i + 1) * rows, :] = in_ref[i].astype(f32)
    half = blocks * rows // 9
    for j in range(9):
        turned = flat_ref[pl.ds(j, half, stride=9), :].T.astype(bf16)
        for i in range(copies):
            if j < 4:
                out_ref[i, 128 * j : 128 * j + 128, 0:half] = turned
            elif j == 4:
                out_ref[i, 512:576, 0:half] = turned[0:64]
                out_ref[i, 0:64, half : 2 * half] = turned[64:128]
            else:
                out_ref[i, 128 * j - 576 : 128 * j - 448, half : 2 * half] = turned


def own_load(flat_ref, pairs):
    low = lax.broadcasted_iota(jnp.int32, (pairs, 128), 1) < 64
    flat = [flat_ref[pl.ds(j, pairs, stride=9), :] for j in range(9)]
    turned = [pltpu.roll(flat[j], 64, 1) for j in range(4, 9)]
    even = flat[:4] + [flat[4]]
    odd = [jnp.where(low, turned[k], turned[k + 1]) for k in range(4)] + [turned[4]]
    return jnp.concatenate([jnp.concatenate(even, 1), jnp.concatenate(odd, 1)], 0)[:, :ROWS]


def own_store(flat_ref, value, pairs):
    value = jnp.concatenate([value, jnp.zeros((2 * pairs, 64), f32)], 1)
    low = lax.broadcasted_iota(jnp.int32, (pairs, 128), 1) < 64
    even = [value[:pairs, 128 * j : 128 * j + 128] for j in range(5)]
    odd = [pltpu.roll(value[pairs:, 128 * j : 128 * j + 128], 64, 1) for j in range(5)]
    flat = even[:4] + [jnp.where(low, even[4], odd[0])]
    flat += [jnp.where(low, odd[k], odd[k + 1]) for k in range(4)]
    for j in range(9):
        flat_ref[pl.ds(j, pairs, stride=9), :] = flat[j]


def gram_kernel(mine_ref, grad_ref, momentum_ref, scale_ref, gram_ref, momentum_out_ref):
    total = None
    for i in range(mine_ref.shape[0]):
        v = mine_ref[i]
        d = lax.dot_general(v, v, NT, preferred_element_type=f32)
        total = d if total is None else total + d
    gram_ref[...] = total
    momentum_out_ref[...] = momentum_rate * momentum_ref[...] + scale_ref[0:1, :] * grad_ref[...]


def iterate_kernel(update_scale, mine_ref, other_ref, gram_ref, own_ref, out_ref, poly_ref, next_ref, flat_ref):
    blocks = [(r, i) for r in (mine_ref, other_ref) for i in range(r.shape[0])]
    pairs = own_ref.shape[0] // 9

    def gram(total, values):
        for get in values:
            v = get()
            d = lax.dot_general(v, v, NT, preferred_element_type=f32)
            total = d if total is None else total + d
        return total

    def poly(gram_matrix):
        low = gram_matrix.astype(bf16)
        squared = jnp.dot(low, low, preferred_element_type=f32)
        return (coef_second * gram_matrix + coef_third * squared).astype(bf16)

    poly_ref[...] = poly(gram(gram_ref[...], [lambda i=i: other_ref[i] for i in range(other_ref.shape[0])]))
    for i, (r, k) in enumerate(blocks):
        v = r[k]
        product = jnp.dot(poly_ref[...], v, preferred_element_type=f32)
        next_ref[i] = (coef_first * v.astype(f32) + product).astype(bf16)
    own = own_load(own_ref, pairs)
    product = jnp.dot(own.astype(bf16), poly_ref[...], preferred_element_type=f32)
    own = (coef_first * own + product).astype(bf16)
    poly_ref[...] = poly(gram(None, [lambda i=i: next_ref[i] for i in range(len(blocks))]))
    product = jnp.dot(own, poly_ref[...], preferred_element_type=f32)
    own_store(flat_ref, update_scale * (coef_first * own.astype(f32) + product), pairs)
    out_ref[0] = flat_ref[...].astype(bf16)


def kernel(body, name, out, in_specs, scratch=(), cost=None):
    return pl.pallas_call(
        body,
        name=name,
        out_shape=out,
        in_specs=in_specs,
        out_specs=jax.tree.map(lambda _: VMEM, out),
        scratch_shapes=list(scratch),
        compiler_params=pltpu.CompilerParams(vmem_limit_bytes=40 * 2**20),
        cost_estimate=cost,
    )


def local(entries, update_scale, sizes, grad, momentum):
    nx, ny, nc, ng = sizes
    rows = grad.shape[1]
    columns = ny * rows * 128 // ROWS
    shape = jax.ShapeDtypeStruct
    group = lax.axis_index("group").astype(jnp.int32).reshape(1)
    grad, momentum, group = lax.optimization_barrier((grad, momentum, group))
    sums, grad, momentum = kernel(
        sums_kernel,
        "sums",
        (shape((nx * ny, 128), f32), shape(grad.shape, f32), shape(grad.shape, f32)),
        [VMEM] * 2,
    )(grad, momentum)
    sums = lax.all_to_all(sums.reshape(-1, 1, 128), ("x", "y"), 0, 0).reshape(-1, 128)
    sums = kernel(functools.partial(combine_kernel, ng), "combine", shape((nc * ng, 128), f32), [SMEM, VMEM])(group, sums)
    sums = lax.all_to_all(sums.reshape(-1, 1, 128), ("core", "group"), 0, 0).reshape(-1, 128)
    iterate, own, scale = kernel(
        functools.partial(scale_kernel, entries),
        "scale",
        (shape((ny, rows, 128), bf16), shape((rows, 128), f32), shape((8, 128), f32)),
        [VMEM] * 3,
    )(sums, grad, momentum)
    gathered = lax.all_to_all(iterate, "y", 0, 0)
    turned = kernel(
        functools.partial(transpose_kernel, nx),
        "turn",
        shape((nx, ROWS, columns), bf16),
        [VMEM],
        scratch=[pltpu.VMEM((ny * rows, 128), f32)],
    )(gathered)
    mine = lax.all_to_all(turned, "x", 0, 0)
    other = lax.ppermute(mine, "core", [(0, 1), (1, 0)])
    gram, momentum_out = kernel(
        gram_kernel,
        "gram",
        (shape((ROWS, ROWS), f32), shape(grad.shape, f32)),
        [VMEM] * 4,
        cost=pl.CostEstimate(flops=2 * ROWS * ROWS * columns * nx, bytes_accessed=2 * ROWS * columns * nx, transcendentals=0),
    )(mine, grad, momentum, scale)
    update = kernel(
        functools.partial(iterate_kernel, update_scale),
        "newton",
        shape(grad.shape, bf16),
        [VMEM] * 4,
        scratch=[
            pltpu.VMEM((ROWS, ROWS), bf16),
            pltpu.VMEM((2 * nx, ROWS, columns), bf16),
            pltpu.VMEM((rows, 128), f32),
        ],
    )(mine, other, gram, own)
    return momentum_out, update


def solution(mesh):
    sizes = (4, 8, 2, 12)
    split_mesh = Mesh(mesh.devices.reshape(sizes), ("x", "y", "core", "group"))
    spec = P("group", ("x", "y", "core"), None)

    def run(grad, momentum):
        entries = grad.size
        layers, flat_rows, _ = grad.shape
        width = flat_rows * 128 // ROWS
        update_scale = 0.2 * math.sqrt(max(ROWS, width))
        return jax.shard_map(
            functools.partial(local, entries, update_scale, sizes),
            mesh=split_mesh,
            in_specs=(spec, spec),
            out_specs=(spec, spec),
            check_vma=False,
        )(grad, momentum)

    return run
```

time: 102 us -> 96.2 us (0.943)
  blocking collectives: 48 us -> 75.6 us
  starting transfers between devices: 23.3 us -> 5.11 us
  waiting for transfers between devices: 13.1 us -> 0.8 us
  local copies, waits for them, and re-layouts: 3.54 us -> 1.76 us
    all_to_all x1 -> x2, blocking collectives: 19.4 us -> 45.4 us  [the longest x1 26.4 us: local(): lax.all_to_all(sums.reshape(-1, 1, 128), ('core', 'group'), 0, 0)]
    all_to_all x1 -> x0, starting transfers between devices: 17.3 us -> none  [local(): sums = lax.all_to_all(sums, ('core', 'group'), 0, 0)]
    all_to_all x1 -> x0, waiting for transfers between devices: 10.7 us -> none  [local(): sums = lax.all_to_all(sums, ('core', 'group'), 0, 0)]
    unnamed x8 -> x4, local copies, waits for them, and re-layouts: 3.53 us -> 1.76 us
    ppermute x1, waiting for transfers between devices: 2.44 us -> 0.8 us  [local(): other = lax.ppermute(mine, 'core', [(0, 1), (1, 0)])]
    pallas_call x1, Pallas kernels: 10.3 us -> 8.73 us  [local(): kernel(functools.partial(iterate_kernel, update_scale), 'newton', shape(g...]
    pallas_call x3 -> x4, Pallas kernels: 2.17 us -> 2.86 us  [the longest x1 1.66 us: local(): kernel(gram_kernel, 'gram', (shape((ROWS, ROWS), f32), shape(grad.shape,...]
  transfers between devices with their start and end apart: 2 -> 1, of which waited for: 2 -> 1; matrix products, arithmetic and copies ran while one was open for 0% -> 0% of each run, Pallas kernels for 0% -> 2%
where the time goes in v2:
time: 96.2 us; the launch traced here: 95.8 us
  blocking collectives  75.6 us (79%)
  Pallas kernels  11.8 us (12%)
  starting transfers between devices  5.11 us (5%)
  local copies, waits for them, and re-layouts  1.76 us (2%)
    all_to_all x1, blocking collectives, local(): lax.all_to_all(sums.reshape(-1, 1, 128), ('core', 'group'), 0, 0)  26.4 us
    all_to_all x1, blocking collectives, local(): lax.all_to_all(sums.reshape(-1, 1, 128), ('x', 'y'), 0, 0).reshape(-1, 128)  18.9 us
    all_to_all x1, blocking collectives, local(): mine = lax.all_to_all(turned, 'x', 0, 0)  16.7 us
    all_to_all x1, blocking collectives, local(): gathered = lax.all_to_all(iterate, 'y', 0, 0)  13.6 us
    pallas_call x1, Pallas kernels, local(): kernel(functools.partial(iterate_kernel, update_scale), 'newton', shape(g...  8.73 us
    ppermute x1, starting transfers between devices, local(): other = lax.ppermute(mine, 'core', [(0, 1), (1, 0)])  5.11 us
  transfers between devices with their start and end apart: 1, of which 1 were waited for; matrix products, arithmetic and copies ran while one was open for 0% of the time, Pallas kernels for 2%

profile of v2, /device:TPU:1, one launch (start us, length us, event | category | flops | bytes accessed | tf_op | source)
XLA Modules:
  0.0 95.8 jit_solution(2605572397032171480)
XLA Ops:
  0.6 0.0 copy-start
  0.6 0.9 copy-done
  1.5 0.0 copy-start.1
  1.5 0.9 copy-done.1
  2.4 0.7 sums.1
  3.2 18.9 %all_to_all.20 = f32[32,1,128]{2,1,0:T(1,128)S(1)} all-to-all(f32[32,1,128]{2,1,0:T(1,128)S(1)} %bitcast.12), channel_id=1, replica_groups=mesh['x'=4,'y'=8,'core'=2,'group'=12] {'x','y'}, dimensions={0} | all-to-all | bytes 32768 | tf_op jit(solution)/shard_map/all_to_all | solution.py:253
  22.1 0.2 combine.1
  22.3 26.4 %all_to_all.21 = f32[24,1,128]{2,1,0:T(1,128)S(1)} all-to-all(f32[24,1,128]{2,1,0:T(1,128)S(1)} %bitcast.11), channel_id=1, replica_groups=mesh['x'=4,'y'=8,'core'=2,'group'=12] {'core','group'}, dimensions={0} | all-to-all | bytes 24576 | tf_op jit(solution)/shard_map/all_to_all | solution.py:255
  48.7 0.3 scale.1
  49.0 13.6 %all_to_all.22.in_ref = bf16[8,144,128]{2,1,0:T(8,128)(2,1)S(1)} all-to-all(bf16[8,144,128]{2,1,0:T(8,128)(2,1)S(1)} %get-tuple-element.19), channel_id=1, replica_groups=mesh['x'=4,'y'=8,'core'=2,'group'=12] {'y'}, dimensions={0} | all-to-all | bytes 589824 | tf_op jit(solution)/shard_map/all_to_all | solution.py:262
  62.6 0.3 turn.1
  62.9 16.7 %all_to_all.23.mine_ref = bf16[4,576,256]{2,1,0:T(8,128)(2,1)S(1)} all-to-all(bf16[4,576,256]{2,1,0:T(8,128)(2,1)S(1)} %turn.1), channel_id=1, replica_groups=mesh['x'=4,'y'=8,'core'=2,'group'=12] {'x'}, dimensions={0} | all-to-all | bytes 2359296 | tf_op jit(solution)/shard_map/all_to_all | solution.py:270
  79.5 5.1 %collective-permute-start = (bf16[4,576,256]{2,1,0:T(8,128)(2,1)S(1)}, bf16[4,576,256]{2,1,0:T(8,128)(2,1)S(1)}, u32[]{:S(2)}, u32[]{:S(2)}) collective-permute-start(bf16[4,576,256]{2,1,0:T(8,128)(2,1)S(1)} %all_to_all.23.mine_ref), channel_id=1, source_target_pairs={{0,12},{12,0},{1,13},{13,1},{2,14},{14,2},{3,15},{15,3},{4,16},{16... | collective-permute-start | bytes 3538952 | tf_op jit(solution)/shard_map/ppermute | solution.py:271
  84.6 1.7 %gram.1 = (f32[576,576]{1,0:T(8,128)S(1)}, f32[1,144,128]{2,1,0:T(8,128)}) custom-call(bf16[4,576,256]{2,1,0:T(8,128)(2,1)S(1)} %all_to_all.23.mine_ref, f32[1,144,128]{2,1,0:T(8,128)S(1)} %get-tuple-element.17.grad_ref, f32[1,144,128]{2,1,0:T(8,128)S(1)} %get-tuple-element.18.momentum_ref, f32[8,128]{1,0:T(8,128)S(1)} %get-tuple-element.20.scale_ref), custom_call_target="tpu_custom_call" | custom-call | flops 679477248 | bytes 1179648 | tf_op jit(solution)/shard_map/gram/pallas_call | solution.py:272
  86.3 0.8 collective-permute-done.other_ref
  87.1 8.7 %newton.1 = bf16[1,144,128]{2,1,0:T(8,128)(2,1)} custom-call(bf16[4,576,256]{2,1,0:T(8,128)(2,1)S(1)} %all_to_all.23.mine_ref, bf16[4,576,256]{2,1,0:T(8,128)(2,1)S(1)} %collective-permute-done.other_ref, f32[576,576]{1,0:T(8,128)S(1)} %get-tuple-element.22.gram_ref, f32[144,128]{1,0:T(8,128)S(1)} %get-tuple-element.23.own_ref), custom_call_target="tpu_custom_call" | custom-call | tf_op jit(solution)/shard_map/newton/pallas_call | solution.py:279
Async XLA Ops:
  0.6 0.9 copy-start
  1.5 0.9 copy-start.1
  79.5 7.6 %collective-permute-start = (bf16[4,576,256]{2,1,0:T(8,128)(2,1)S(1)}, bf16[4,576,256]{2,1,0:T(8,128)(2,1)S(1)}, u32[]{:S(2)}, u32[]{:S(2)}) collective-permute-start(bf16[4,576,256]{2,1,0:T(8,128)(2,1)S(1)} %all_to_all.23.mine_ref), channel_id=1, source_target_pairs={{0,12},{12,0},{1,13},{13,1},{2,14},{14,2},{3,15},{15,3},{4,16},{16... | collective-permute-start | bytes 3538952 | tf_op jit(solution)/shard_map/ppermute | solution.py:271

commit v3 on v2

--- a/solution.py
+++ b/solution.py
@@ -94,13 +94,11 @@
     return fast_two_sum(high, low + pltpu.roll(high, 64, 1))
 
 
-def sums_kernel(grad_ref, momentum_ref, out_ref, grad_out_ref, momentum_out_ref):
-    grad_out_ref[...] = grad_ref[...]
-    momentum_out_ref[...] = momentum_ref[...]
+def sums_kernel(pair_ref, out_ref):
     gg, gm, mm = [], [], []
-    for i in range(0, grad_ref.shape[1], 8):
-        g = grad_ref[0, i : i + 8, :]
-        m = momentum_ref[0, i : i + 8, :]
+    for i in range(0, pair_ref.shape[1], 8):
+        g = pair_ref[0, i : i + 8, :]
+        m = pair_ref[1, i : i + 8, :]
         gg.append(two_prod(g, g))
         gm.append(two_prod(g, m))
         mm.append(two_prod(m, m))
@@ -120,7 +118,7 @@
         out_ref[i : i + 8, :] = jnp.where(keep, tile, 0.0)
 
 
-def scale_kernel(entries, in_ref, grad_ref, momentum_ref, out_ref, own_ref, scale_ref):
+def scale_kernel(entries, in_ref, pair_ref, out_ref, own_ref, scale_ref):
     high, low = add_rows(in_ref)
     lane = lanes()
 
@@ -138,8 +136,8 @@
     cross = dd_mul(dd_mul((2.0 * a[0], 2.0 * a[1]), b), gm)
     total = dd_add(dd_add(dd_mul(a, dd_mul(a, gg)), dd_mul(dd_mul(b, b), mm)), cross)
     unorm = jnp.sqrt(jnp.maximum(total[0], 0.0))
-    scaled_grad = grad_scale * grad_ref[0]
-    nudged = scaled_grad + momentum_rate * (momentum_rate * momentum_ref[0] + scaled_grad)
+    scaled_grad = grad_scale * pair_ref[0]
+    nudged = scaled_grad + momentum_rate * (momentum_rate * pair_ref[1] + scaled_grad)
     iterate = (nudged / (unorm + 1e-07)).astype(bf16)
     for i in range(out_ref.shape[0]):
         out_ref[i] = iterate
@@ -184,33 +182,45 @@
         flat_ref[pl.ds(j, pairs, stride=9), :] = flat[j]
 
 
-def gram_kernel(mine_ref, grad_ref, momentum_ref, scale_ref, gram_ref, momentum_out_ref):
-    total = None
-    for i in range(mine_ref.shape[0]):
-        v = mine_ref[i]
-        d = lax.dot_general(v, v, NT, preferred_element_type=f32)
-        total = d if total is None else total + d
-    gram_ref[...] = total
-    momentum_out_ref[...] = momentum_rate * momentum_ref[...] + scale_ref[0:1, :] * grad_ref[...]
-
-
-def iterate_kernel(update_scale, mine_ref, other_ref, gram_ref, own_ref, out_ref, poly_ref, next_ref, flat_ref):
+def triangle():
+    return [(a, min(a + 256, ROWS)) for a in range(0, ROWS, 256)]
+
+
+def side_by_side(values):
+    return jnp.concatenate(values, 1)
+
+
+def gram_columns(iterate):
+    return [lax.dot_general(iterate[a:], iterate[a:b], NT, preferred_element_type=f32) for a, b in triangle()]
+
+
+def mirror(ref, value, a, b):
+    ref[a:, a:b] = value
+    if b < ROWS:
+        ref[a:b, b:] = value[b - a :].T
+
+
+def store_poly(columns, low_ref, poly_ref):
+    for (a, b), column in zip(triangle(), columns):
+        mirror(low_ref, column.astype(bf16), a, b)
+    for (a, b), column in zip(triangle(), columns):
+        squared = jnp.dot(low_ref[a:, :], low_ref[:, a:b], preferred_element_type=f32)
+        mirror(poly_ref, (coef_second * column + coef_third * squared).astype(bf16), a, b)
+
+
+def gram_kernel(mine_ref, pair_ref, scale_ref, gram_ref, momentum_out_ref):
+    iterate = side_by_side([mine_ref[i] for i in range(mine_ref.shape[0])])
+    for (a, b), column in zip(triangle(), gram_columns(iterate)):
+        gram_ref[a:, a:b] = column
+    momentum_out_ref[0] = momentum_rate * pair_ref[1] + scale_ref[0:1, :] * pair_ref[0]
+
+
+def iterate_kernel(update_scale, mine_ref, other_ref, gram_ref, own_ref, out_ref, poly_ref, next_ref, flat_ref, low_ref):
     blocks = [(r, i) for r in (mine_ref, other_ref) for i in range(r.shape[0])]
     pairs = own_ref.shape[0] // 9
-
-    def gram(total, values):
-        for get in values:
-            v = get()
-            d = lax.dot_general(v, v, NT, preferred_element_type=f32)
-            total = d if total is None else total + d
-        return total
-
-    def poly(gram_matrix):
-        low = gram_matrix.astype(bf16)
-        squared = jnp.dot(low, low, preferred_element_type=f32)
-        return (coef_second * gram_matrix + coef_third * squared).astype(bf16)
-
-    poly_ref[...] = poly(gram(gram_ref[...], [lambda i=i: other_ref[i] for i in range(other_ref.shape[0])]))
+    columns = gram_columns(side_by_side([other_ref[i] for i in range(other_ref.shape[0])]))
+    columns = [gram_ref[a:, a:b] + column for (a, b), column in zip(triangle(), columns)]
+    store_poly(columns, low_ref, poly_ref)
     for i, (r, k) in enumerate(blocks):
         v = r[k]
         product = jnp.dot(poly_ref[...], v, preferred_element_type=f32)
@@ -218,7 +228,7 @@
     own = own_load(own_ref, pairs)
     product = jnp.dot(own.astype(bf16), poly_ref[...], preferred_element_type=f32)
     own = (coef_first * own + product).astype(bf16)
-    poly_ref[...] = poly(gram(None, [lambda i=i: next_ref[i] for i in range(len(blocks))]))
+    store_poly(gram_columns(side_by_side([next_ref[i] for i in range(len(blocks))])), low_ref, poly_ref)
     product = jnp.dot(own, poly_ref[...], preferred_element_type=f32)
     own_store(flat_ref, update_scale * (coef_first * own.astype(f32) + product), pairs)
     out_ref[0] = flat_ref[...].astype(bf16)
@@ -244,21 +254,18 @@
     shape = jax.ShapeDtypeStruct
     group = lax.axis_index("group").astype(jnp.int32).reshape(1)
     grad, momentum, group = lax.optimization_barrier((grad, momentum, group))
-    sums, grad, momentum = kernel(
-        sums_kernel,
-        "sums",
-        (shape((nx * ny, 128), f32), shape(grad.shape, f32), shape(grad.shape, f32)),
-        [VMEM] * 2,
-    )(grad, momentum)
-    sums = lax.all_to_all(sums.reshape(-1, 1, 128), ("x", "y"), 0, 0).reshape(-1, 128)
-    sums = kernel(functools.partial(combine_kernel, ng), "combine", shape((nc * ng, 128), f32), [SMEM, VMEM])(group, sums)
-    sums = lax.all_to_all(sums.reshape(-1, 1, 128), ("core", "group"), 0, 0).reshape(-1, 128)
+    first = lax.broadcasted_iota(jnp.int32, (2, rows, 128), 0) == 0
+    pair = jnp.where(first, grad, momentum)
+    sums = kernel(sums_kernel, "sums", shape((ny * nc, 128), f32), [VMEM])(pair)
+    sums = lax.all_to_all(sums.reshape(-1, 1, 128), ("y", "core"), 0, 0).reshape(-1, 128)
+    sums = kernel(functools.partial(combine_kernel, ng), "combine", shape((nx * ng, 128), f32), [SMEM, VMEM])(group, sums)
+    sums = lax.all_to_all(sums.reshape(-1, 1, 128), ("x", "group"), 0, 0).reshape(-1, 128)
     iterate, own, scale = kernel(
         functools.partial(scale_kernel, entries),
         "scale",
         (shape((ny, rows, 128), bf16), shape((rows, 128), f32), shape((8, 128), f32)),
-        [VMEM] * 3,
-    )(sums, grad, momentum)
+        [VMEM] * 2,
+    )(sums, pair)
     gathered = lax.all_to_all(iterate, "y", 0, 0)
     turned = kernel(
         functools.partial(transpose_kernel, nx),
@@ -273,9 +280,9 @@
         gram_kernel,
         "gram",
         (shape((ROWS, ROWS), f32), shape(grad.shape, f32)),
-        [VMEM] * 4,
+        [VMEM] * 3,
         cost=pl.CostEstimate(flops=2 * ROWS * ROWS * columns * nx, bytes_accessed=2 * ROWS * columns * nx, transcendentals=0),
-    )(mine, grad, momentum, scale)
+    )(mine, pair, scale)
     update = kernel(
         functools.partial(iterate_kernel, update_scale),
         "newton",
@@ -285,6 +292,7 @@
             pltpu.VMEM((ROWS, ROWS), bf16),
             pltpu.VMEM((2 * nx, ROWS, columns), bf16),
             pltpu.VMEM((rows, 128), f32),
+            pltpu.VMEM((ROWS, ROWS), bf16),
         ],
     )(mine, other, gram, own)
     return momentum_out, update

time: 96.2 us -> 89.9 us (0.935)
  blocking collectives: 75.6 us -> 70.5 us
  Pallas kernels: 11.8 us -> 8.91 us
  starting transfers between devices: 5.11 us -> 7.3 us
  local copies, waits for them, and re-layouts: 1.76 us -> 0 us
  other arithmetic: 0 us -> 1.01 us
    pallas_call x1, Pallas kernels: 8.73 us -> 6.17 us  [local(): kernel(functools.partial(iterate_kernel, update_scale), 'newton', shape(g...]
    ppermute x1, starting transfers between devices: 5.11 us -> 7.3 us  [local(): other = lax.ppermute(mine, 'core', [(0, 1), (1, 0)])]
    all_to_all x1, blocking collectives: 16.7 us -> 14.5 us  [local(): mine = lax.all_to_all(turned, 'x', 0, 0)]
    all_to_all x1, blocking collectives: 13.6 us -> 11.7 us  [local(): gathered = lax.all_to_all(iterate, 'y', 0, 0)]
    unnamed x4 -> x0, local copies, waits for them, and re-layouts: 1.76 us -> none
    select_n x0 -> x1, other arithmetic: none -> 1 us  [local(): pair = jnp.where(first, grad, momentum)]
    all_to_all x2, blocking collectives: 45.4 us -> 44.4 us  [the longest x1 24.4 us: local(): lax.all_to_all(sums.reshape(-1, 1, 128), ('x', 'group'), 0, 0)]
  transfers between devices with their start and end apart: 1 -> 1, of which waited for: 1 -> 1; matrix products, arithmetic and copies ran while one was open for 0% -> 0% of each run, Pallas kernels for 2% -> 1%
where the time goes in v3:
time: 89.9 us; the launch traced here: 89.6 us
  blocking collectives  70.5 us (78%)
  Pallas kernels  8.91 us (10%)
  starting transfers between devices  7.3 us (8%)
  waiting for transfers between devices  1.17 us (1%)
  other arithmetic  1.01 us (1%)
    all_to_all x1, blocking collectives, local(): lax.all_to_all(sums.reshape(-1, 1, 128), ('x', 'group'), 0, 0)  24.4 us
    all_to_all x1, blocking collectives, local(): lax.all_to_all(sums.reshape(-1, 1, 128), ('y', 'core'), 0, 0)  20 us
    all_to_all x1, blocking collectives, local(): mine = lax.all_to_all(turned, 'x', 0, 0)  14.5 us
    all_to_all x1, blocking collectives, local(): gathered = lax.all_to_all(iterate, 'y', 0, 0)  11.7 us
    ppermute x1, starting transfers between devices, local(): other = lax.ppermute(mine, 'core', [(0, 1), (1, 0)])  7.3 us
    pallas_call x1, Pallas kernels, local(): kernel(functools.partial(iterate_kernel, update_scale), 'newton', shape(g...  6.17 us
  transfers between devices with their start and end apart: 1, of which 1 were waited for; matrix products, arithmetic and copies ran while one was open for 0% of the time, Pallas kernels for 1%

profile of v3, /device:TPU:1, one launch (start us, length us, event | category | flops | bytes accessed | tf_op | source)
XLA Modules:
  0.0 89.6 jit_solution(5508856112977360416)
XLA Ops:
  0.7 1.0 %broadcast_select_fusion.pair_ref = f32[2,144,128]{2,1,0:T(8,128)S(1)} fusion(f32[144,128]{1,0:T(8,128)} %bitcast.15, f32[144,128]{1,0:T(8,128)} %bitcast.16, pred[2]{0:T(512)(128)(4,1)S(1)} %iota_compare_fusion), kind=kLoop, calls=%fused_computation | loop fusion | flops 36864 | bytes 294914 | tf_op jit(solution)/shard_map/jit(_where)/select_n | solution.py:258
  1.7 0.7 sums.1
  2.4 20.0 %all_to_all.20 = f32[16,1,128]{2,1,0:T(1,128)S(1)} all-to-all(f32[16,1,128]{2,1,0:T(1,128)S(1)} %bitcast.13), channel_id=1, replica_groups=mesh['x'=4,'y'=8,'core'=2,'group'=12] {'y','core'}, dimensions={0} | all-to-all | bytes 16384 | tf_op jit(solution)/shard_map/all_to_all | solution.py:260
  22.4 0.2 combine.1
  22.5 24.4 %all_to_all.21 = f32[48,1,128]{2,1,0:T(1,128)S(1)} all-to-all(f32[48,1,128]{2,1,0:T(1,128)S(1)} %bitcast.11), channel_id=1, replica_groups=mesh['x'=4,'y'=8,'core'=2,'group'=12] {'x','group'}, dimensions={0} | all-to-all | bytes 49152 | tf_op jit(solution)/shard_map/all_to_all | solution.py:262
  46.9 0.3 scale.1
  47.2 11.7 %all_to_all.22.in_ref = bf16[8,144,128]{2,1,0:T(8,128)(2,1)S(1)} all-to-all(bf16[8,144,128]{2,1,0:T(8,128)(2,1)S(1)} %get-tuple-element.13), channel_id=1, replica_groups=mesh['x'=4,'y'=8,'core'=2,'group'=12] {'y'}, dimensions={0} | all-to-all | bytes 589824 | tf_op jit(solution)/shard_map/all_to_all | solution.py:269
  58.9 0.3 turn.1
  59.2 14.5 %all_to_all.23.mine_ref = bf16[4,576,256]{2,1,0:T(8,128)(2,1)S(1)} all-to-all(bf16[4,576,256]{2,1,0:T(8,128)(2,1)S(1)} %turn.1), channel_id=1, replica_groups=mesh['x'=4,'y'=8,'core'=2,'group'=12] {'x'}, dimensions={0} | all-to-all | bytes 2359296 | tf_op jit(solution)/shard_map/all_to_all | solution.py:277
  73.7 7.3 %collective-permute-start = (bf16[4,576,256]{2,1,0:T(8,128)(2,1)S(1)}, bf16[4,576,256]{2,1,0:T(8,128)(2,1)S(1)}, u32[]{:S(2)}, u32[]{:S(2)}) collective-permute-start(bf16[4,576,256]{2,1,0:T(8,128)(2,1)S(1)} %all_to_all.23.mine_ref), channel_id=1, source_target_pairs={{0,12},{12,0},{1,13},{13,1},{2,14},{14,2},{3,15},{15,3},{4,16},{16... | collective-permute-start | bytes 3538952 | tf_op jit(solution)/shard_map/ppermute | solution.py:278
  81.0 1.3 %gram.1 = (f32[576,576]{1,0:T(8,128)S(1)}, f32[1,144,128]{2,1,0:T(8,128)}) custom-call(bf16[4,576,256]{2,1,0:T(8,128)(2,1)S(1)} %all_to_all.23.mine_ref, f32[2,144,128]{2,1,0:T(8,128)S(1)} %broadcast_select_fusion.pair_ref, f32[8,128]{1,0:T(8,128)S(1)} %get-tuple-element.14.scale_ref), custom_call_target="tpu_custom_call" | custom-call | flops 679477248 | bytes 1179648 | tf_op jit(solution)/shard_map/gram/pallas_call | solution.py:279
  82.3 1.2 %collective-permute-done.other_ref = bf16[4,576,256]{2,1,0:T(8,128)(2,1)S(1)} collective-permute-done((bf16[4,576,256]{2,1,0:T(8,128)(2,1)S(1)}, bf16[4,576,256]{2,1,0:T(8,128)(2,1)S(1)}, u32[]{:S(2)}, u32[]{:S(2)}) %collective-permute-start) | collective-permute-done | bytes 1179680 | tf_op jit(solution)/shard_map/ppermute | solution.py:278
  83.4 6.2 %newton.1 = bf16[1,144,128]{2,1,0:T(8,128)(2,1)} custom-call(bf16[4,576,256]{2,1,0:T(8,128)(2,1)S(1)} %all_to_all.23.mine_ref, bf16[4,576,256]{2,1,0:T(8,128)(2,1)S(1)} %collective-permute-done.other_ref, f32[576,576]{1,0:T(8,128)S(1)} %get-tuple-element.16.gram_ref, f32[144,128]{1,0:T(8,128)S(1)} %get-tuple-element.17.own_ref), custom_call_target="tpu_custom_call" | custom-call | tf_op jit(solution)/shard_map/newton/pallas_call | solution.py:286
  (1 shorter events, 0.0 us)
Async XLA Ops:
  73.7 9.8 %collective-permute-start = (bf16[4,576,256]{2,1,0:T(8,128)(2,1)S(1)}, bf16[4,576,256]{2,1,0:T(8,128)(2,1)S(1)}, u32[]{:S(2)}, u32[]{:S(2)}) collective-permute-start(bf16[4,576,256]{2,1,0:T(8,128)(2,1)S(1)} %all_to_all.23.mine_ref), channel_id=1, source_target_pairs={{0,12},{12,0},{1,13},{13,1},{2,14},{14,2},{3,15},{15,3},{4,16},{16... | collective-permute-start | bytes 3538952 | tf_op jit(solution)/shard_map/ppermute | solution.py:278

commit v4 on v3

--- a/solution.py
+++ b/solution.py
@@ -216,13 +216,12 @@
 
 
 def iterate_kernel(update_scale, mine_ref, other_ref, gram_ref, own_ref, out_ref, poly_ref, next_ref, flat_ref, low_ref):
-    blocks = [(r, i) for r in (mine_ref, other_ref) for i in range(r.shape[0])]
+    blocks = [side_by_side([r[i], r[i + 1]]) for r in (mine_ref, other_ref) for i in range(0, r.shape[0], 2)]
     pairs = own_ref.shape[0] // 9
     columns = gram_columns(side_by_side([other_ref[i] for i in range(other_ref.shape[0])]))
     columns = [gram_ref[a:, a:b] + column for (a, b), column in zip(triangle(), columns)]
     store_poly(columns, low_ref, poly_ref)
-    for i, (r, k) in enumerate(blocks):
-        v = r[k]
+    for i, v in enumerate(blocks):
         product = jnp.dot(poly_ref[...], v, preferred_element_type=f32)
         next_ref[i] = (coef_first * v.astype(f32) + product).astype(bf16)
     own = own_load(own_ref, pairs)
@@ -248,40 +247,41 @@
 
 
 def local(entries, update_scale, sizes, grad, momentum):
-    nx, ny, nc, ng = sizes
+    nx, nh, nl, nc, ng = sizes
     rows = grad.shape[1]
-    columns = ny * rows * 128 // ROWS
+    columns = nh * rows * 128 // ROWS
+    copies = nx * nl
     shape = jax.ShapeDtypeStruct
     group = lax.axis_index("group").astype(jnp.int32).reshape(1)
     grad, momentum, group = lax.optimization_barrier((grad, momentum, group))
     first = lax.broadcasted_iota(jnp.int32, (2, rows, 128), 0) == 0
     pair = jnp.where(first, grad, momentum)
-    sums = kernel(sums_kernel, "sums", shape((ny * nc, 128), f32), [VMEM])(pair)
-    sums = lax.all_to_all(sums.reshape(-1, 1, 128), ("y", "core"), 0, 0).reshape(-1, 128)
+    sums = kernel(sums_kernel, "sums", shape((nh * nl * nc, 128), f32), [VMEM])(pair)
+    sums = lax.all_to_all(sums.reshape(-1, 1, 128), ("yh", "yl", "core"), 0, 0).reshape(-1, 128)
     sums = kernel(functools.partial(combine_kernel, ng), "combine", shape((nx * ng, 128), f32), [SMEM, VMEM])(group, sums)
     sums = lax.all_to_all(sums.reshape(-1, 1, 128), ("x", "group"), 0, 0).reshape(-1, 128)
     iterate, own, scale = kernel(
         functools.partial(scale_kernel, entries),
         "scale",
-        (shape((ny, rows, 128), bf16), shape((rows, 128), f32), shape((8, 128), f32)),
+        (shape((nh, rows, 128), bf16), shape((rows, 128), f32), shape((8, 128), f32)),
         [VMEM] * 2,
     )(sums, pair)
-    gathered = lax.all_to_all(iterate, "y", 0, 0)
+    gathered = lax.all_to_all(iterate, "yh", 0, 0)
     turned = kernel(
-        functools.partial(transpose_kernel, nx),
+        functools.partial(transpose_kernel, copies),
         "turn",
-        shape((nx, ROWS, columns), bf16),
+        shape((copies, ROWS, columns), bf16),
         [VMEM],
-        scratch=[pltpu.VMEM((ny * rows, 128), f32)],
+        scratch=[pltpu.VMEM((nh * rows, 128), f32)],
     )(gathered)
-    mine = lax.all_to_all(turned, "x", 0, 0)
+    mine = lax.all_to_all(turned, ("x", "yl"), 0, 0)
     other = lax.ppermute(mine, "core", [(0, 1), (1, 0)])
     gram, momentum_out = kernel(
         gram_kernel,
         "gram",
         (shape((ROWS, ROWS), f32), shape(grad.shape, f32)),
         [VMEM] * 3,
-        cost=pl.CostEstimate(flops=2 * ROWS * ROWS * columns * nx, bytes_accessed=2 * ROWS * columns * nx, transcendentals=0),
+        cost=pl.CostEstimate(flops=2 * ROWS * ROWS * columns * copies, bytes_accessed=2 * ROWS * columns * copies, transcendentals=0),
     )(mine, pair, scale)
     update = kernel(
         functools.partial(iterate_kernel, update_scale),
@@ -290,7 +290,7 @@
         [VMEM] * 4,
         scratch=[
             pltpu.VMEM((ROWS, ROWS), bf16),
-            pltpu.VMEM((2 * nx, ROWS, columns), bf16),
+            pltpu.VMEM((copies, ROWS, 2 * columns), bf16),
             pltpu.VMEM((rows, 128), f32),
             pltpu.VMEM((ROWS, ROWS), bf16),
         ],
@@ -299,9 +299,9 @@
 
 
 def solution(mesh):
-    sizes = (4, 8, 2, 12)
-    split_mesh = Mesh(mesh.devices.reshape(sizes), ("x", "y", "core", "group"))
-    spec = P("group", ("x", "y", "core"), None)
+    sizes = (4, 4, 2, 2, 12)
+    split_mesh = Mesh(mesh.devices.reshape(sizes), ("x", "yh", "yl", "core", "group"))
+    spec = P("group", ("x", "yh", "yl", "core"), None)
 
     def run(grad, momentum):
         entries = grad.size

time: 89.9 us -> 89 us (0.990)
  no operation moved by 1% of the time
where the time goes in v4:
time: 89 us; the launch traced here: 88.7 us
  blocking collectives  70.1 us (79%)
  Pallas kernels  9.18 us (10%)
  starting transfers between devices  6.55 us (7%)
  waiting for transfers between devices  1.17 us (1%)
  other arithmetic  1.01 us (1%)
    all_to_all x1, blocking collectives, local(): lax.all_to_all(sums.reshape(-1, 1, 128), ('x', 'group'), 0, 0)  24.4 us
    all_to_all x1, blocking collectives, local(): lax.all_to_all(sums.reshape(-1, 1, 128), ('yh', 'yl', 'core'), 0, 0)  20 us
    all_to_all x1, blocking collectives, local(): mine = lax.all_to_all(turned, ('x', 'yl'), 0, 0)  15.9 us
    all_to_all x1, blocking collectives, local(): gathered = lax.all_to_all(iterate, 'yh', 0, 0)  9.84 us
    ppermute x1, starting transfers between devices, local(): other = lax.ppermute(mine, 'core', [(0, 1), (1, 0)])  6.55 us
    pallas_call x1, Pallas kernels, local(): kernel(functools.partial(iterate_kernel, update_scale), 'newton', shape(g...  6.18 us
  transfers between devices with their start and end apart: 1, of which 1 were waited for; matrix products, arithmetic and copies ran while one was open for 0% of the time, Pallas kernels for 1%

profile of v4, /device:TPU:1, one launch (start us, length us, event | category | flops | bytes accessed | tf_op | source)
XLA Modules:
  0.0 88.7 jit_solution(12672729427953742159)
XLA Ops:
  0.7 1.0 %broadcast_select_fusion.pair_ref = f32[2,144,128]{2,1,0:T(8,128)S(1)} fusion(f32[144,128]{1,0:T(8,128)} %bitcast.15, f32[144,128]{1,0:T(8,128)} %bitcast.16, pred[2]{0:T(512)(128)(4,1)S(1)} %iota_compare_fusion), kind=kLoop, calls=%fused_computation | loop fusion | flops 36864 | bytes 294914 | tf_op jit(solution)/shard_map/jit(_where)/select_n | solution.py:258
  1.7 0.7 sums.1
  2.4 20.0 %all_to_all.20 = f32[16,1,128]{2,1,0:T(1,128)S(1)} all-to-all(f32[16,1,128]{2,1,0:T(1,128)S(1)} %bitcast.13), channel_id=1, replica_groups=mesh['x'=4,'yh'=4,'yl'=2,'core'=2,'group'=12] {'yh','yl','core'}, dimensions={0} | all-to-all | bytes 16384 | tf_op jit(solution)/shard_map/all_to_all | solution.py:260
  22.4 0.2 combine.1
  22.5 24.4 %all_to_all.21 = f32[48,1,128]{2,1,0:T(1,128)S(1)} all-to-all(f32[48,1,128]{2,1,0:T(1,128)S(1)} %bitcast.11), channel_id=1, replica_groups=mesh['x'=4,'yh'=4,'yl'=2,'core'=2,'group'=12] {'x','group'}, dimensions={0} | all-to-all | bytes 49152 | tf_op jit(solution)/shard_map/all_to_all | solution.py:262
  46.9 0.3 scale.1
  47.2 9.8 %all_to_all.22.in_ref = bf16[4,144,128]{2,1,0:T(8,128)(2,1)S(1)} all-to-all(bf16[4,144,128]{2,1,0:T(8,128)(2,1)S(1)} %get-tuple-element.13), channel_id=1, replica_groups=mesh['x'=4,'yh'=4,'yl'=2,'core'=2,'group'=12] {'yh'}, dimensions={0} | all-to-all | bytes 294912 | tf_op jit(solution)/shard_map/all_to_all | solution.py:269
  57.1 0.5 turn.1
  57.6 15.9 %all_to_all.23.mine_ref = bf16[8,576,128]{2,1,0:T(8,128)(2,1)S(1)} all-to-all(bf16[8,576,128]{2,1,0:T(8,128)(2,1)S(1)} %turn.1), channel_id=1, replica_groups=mesh['x'=4,'yh'=4,'yl'=2,'core'=2,'group'=12] {'x','yl'}, dimensions={0} | all-to-all | bytes 2359296 | tf_op jit(solution)/shard_map/all_to_all | solution.py:277
  73.5 6.6 %collective-permute-start = (bf16[8,576,128]{2,1,0:T(8,128)(2,1)S(1)}, bf16[8,576,128]{2,1,0:T(8,128)(2,1)S(1)}, u32[]{:S(2)}, u32[]{:S(2)}) collective-permute-start(bf16[8,576,128]{2,1,0:T(8,128)(2,1)S(1)} %all_to_all.23.mine_ref), channel_id=1, source_target_pairs={{0,12},{12,0},{1,13},{13,1},{2,14},{14,2},{3,15},{15,3},{4,16},{16... | collective-permute-start | bytes 3538952 | tf_op jit(solution)/shard_map/ppermute | solution.py:278
  80.1 1.3 %gram.1 = (f32[576,576]{1,0:T(8,128)S(1)}, f32[1,144,128]{2,1,0:T(8,128)}) custom-call(bf16[8,576,128]{2,1,0:T(8,128)(2,1)S(1)} %all_to_all.23.mine_ref, f32[2,144,128]{2,1,0:T(8,128)S(1)} %broadcast_select_fusion.pair_ref, f32[8,128]{1,0:T(8,128)S(1)} %get-tuple-element.14.scale_ref), custom_call_target="tpu_custom_call" | custom-call | flops 679477248 | bytes 1179648 | tf_op jit(solution)/shard_map/gram/pallas_call | solution.py:279
  81.4 1.2 %collective-permute-done.other_ref = bf16[8,576,128]{2,1,0:T(8,128)(2,1)S(1)} collective-permute-done((bf16[8,576,128]{2,1,0:T(8,128)(2,1)S(1)}, bf16[8,576,128]{2,1,0:T(8,128)(2,1)S(1)}, u32[]{:S(2)}, u32[]{:S(2)}) %collective-permute-start) | collective-permute-done | bytes 1179680 | tf_op jit(solution)/shard_map/ppermute | solution.py:278
  82.5 6.2 %newton.1 = bf16[1,144,128]{2,1,0:T(8,128)(2,1)} custom-call(bf16[8,576,128]{2,1,0:T(8,128)(2,1)S(1)} %all_to_all.23.mine_ref, bf16[8,576,128]{2,1,0:T(8,128)(2,1)S(1)} %collective-permute-done.other_ref, f32[576,576]{1,0:T(8,128)S(1)} %get-tuple-element.16.gram_ref, f32[144,128]{1,0:T(8,128)S(1)} %get-tuple-element.17.own_ref), custom_call_target="tpu_custom_call" | custom-call | tf_op jit(solution)/shard_map/newton/pallas_call | solution.py:286
  (1 shorter events, 0.0 us)
Async XLA Ops:
  73.5 9.0 %collective-permute-start = (bf16[8,576,128]{2,1,0:T(8,128)(2,1)S(1)}, bf16[8,576,128]{2,1,0:T(8,128)(2,1)S(1)}, u32[]{:S(2)}, u32[]{:S(2)}) collective-permute-start(bf16[8,576,128]{2,1,0:T(8,128)(2,1)S(1)} %all_to_all.23.mine_ref), channel_id=1, source_target_pairs={{0,12},{12,0},{1,13},{13,1},{2,14},{14,2},{3,15},{15,3},{4,16},{16... | collective-permute-start | bytes 3538952 | tf_op jit(solution)/shard_map/ppermute | solution.py:278

commit v5 on v3

--- a/solution.py
+++ b/solution.py
@@ -234,6 +234,25 @@
     out_ref[0] = flat_ref[...].astype(bf16)
 
 
+def pairings(count, core):
+    return [((i + core) % count, (i + core + 1) % count) for i in range(0, count, 2)]
+
+
+def gather_groups(nx, ny, nc):
+    def at(x, y, core):
+        return (x * ny + y) * nc + core
+
+    first, second = [], []
+    for core in range(nc):
+        for xs in pairings(nx, core):
+            for parity in range(2):
+                first.append([at(x, y, core) for x in xs for y in range(parity, ny, 2)])
+        for xs in pairings(nx, 1 - core):
+            for ys in pairings(ny, core):
+                second.append([at(x, y, core) for x in xs for y in ys])
+    return first, second
+
+
 def kernel(body, name, out, in_specs, scratch=(), cost=None):
     return pl.pallas_call(
         body,
@@ -249,8 +268,11 @@
 
 def local(entries, update_scale, sizes, grad, momentum):
     nx, ny, nc, ng = sizes
+    chips = ("x", "y", "core")
+    first_groups, second_groups = gather_groups(nx, ny, nc)
+    blocks, copies = len(first_groups[0]), len(second_groups[0])
     rows = grad.shape[1]
-    columns = ny * rows * 128 // ROWS
+    columns = blocks * rows * 128 // ROWS
     shape = jax.ShapeDtypeStruct
     group = lax.axis_index("group").astype(jnp.int32).reshape(1)
     grad, momentum, group = lax.optimization_barrier((grad, momentum, group))
@@ -263,25 +285,25 @@
     iterate, own, scale = kernel(
         functools.partial(scale_kernel, entries),
         "scale",
-        (shape((ny, rows, 128), bf16), shape((rows, 128), f32), shape((8, 128), f32)),
+        (shape((blocks, rows, 128), bf16), shape((rows, 128), f32), shape((8, 128), f32)),
         [VMEM] * 2,
     )(sums, pair)
-    gathered = lax.all_to_all(iterate, "y", 0, 0)
+    gathered = lax.all_to_all(iterate, chips, 0, 0, axis_index_groups=first_groups)
     turned = kernel(
-        functools.partial(transpose_kernel, nx),
+        functools.partial(transpose_kernel, copies),
         "turn",
-        shape((nx, ROWS, columns), bf16),
+        shape((copies, ROWS, columns), bf16),
         [VMEM],
-        scratch=[pltpu.VMEM((ny * rows, 128), f32)],
+        scratch=[pltpu.VMEM((blocks * rows, 128), f32)],
     )(gathered)
-    mine = lax.all_to_all(turned, "x", 0, 0)
+    mine = lax.all_to_all(turned, chips, 0, 0, axis_index_groups=second_groups)
     other = lax.ppermute(mine, "core", [(0, 1), (1, 0)])
     gram, momentum_out = kernel(
         gram_kernel,
         "gram",
         (shape((ROWS, ROWS), f32), shape(grad.shape, f32)),
         [VMEM] * 3,
-        cost=pl.CostEstimate(flops=2 * ROWS * ROWS * columns * nx, bytes_accessed=2 * ROWS * columns * nx, transcendentals=0),
+        cost=pl.CostEstimate(flops=2 * ROWS * ROWS * columns * copies, bytes_accessed=2 * ROWS * columns * copies, transcendentals=0),
     )(mine, pair, scale)
     update = kernel(
         functools.partial(iterate_kernel, update_scale),
@@ -290,7 +312,7 @@
         [VMEM] * 4,
         scratch=[
             pltpu.VMEM((ROWS, ROWS), bf16),
-            pltpu.VMEM((2 * nx, ROWS, columns), bf16),
+            pltpu.VMEM((2 * copies, ROWS, columns), bf16),
             pltpu.VMEM((rows, 128), f32),
             pltpu.VMEM((ROWS, ROWS), bf16),
         ],

time: 89.9 us -> 89.3 us (level)
  starting transfers between devices: 7.3 us -> 5.45 us
  blocking collectives: 70.5 us -> 71.7 us
    ppermute x1, starting transfers between devices: 7.3 us -> 5.45 us  [local(): other = lax.ppermute(mine, 'core', [(0, 1), (1, 0)])]
    all_to_all x2, blocking collectives: 26.2 us -> 27.4 us  [the longest x1 14.5 us: local(): lax.all_to_all(iterate, chips, 0, 0, axis_index_groups=first_groups)]
where the time goes in v5:
time: 89.3 us; the launch traced here: 88.9 us
  blocking collectives  71.7 us (80%)
  Pallas kernels  8.91 us (10%)
  starting transfers between devices  5.45 us (6%)
  waiting for transfers between devices  1.17 us (1%)
  other arithmetic  1.01 us (1%)
    all_to_all x1, blocking collectives, local(): lax.all_to_all(sums.reshape(-1, 1, 128), ('x', 'group'), 0, 0)  24.4 us
    all_to_all x1, blocking collectives, local(): lax.all_to_all(sums.reshape(-1, 1, 128), ('y', 'core'), 0, 0)  20 us
    all_to_all x1, blocking collectives, local(): lax.all_to_all(iterate, chips, 0, 0, axis_index_groups=first_groups)  14.5 us
    all_to_all x1, blocking collectives, local(): mine = lax.all_to_all(turned, chips, 0, 0, axis_index_groups=second_groups)  12.9 us
    pallas_call x1, Pallas kernels, local(): kernel(functools.partial(iterate_kernel, update_scale), 'newton', shape(g...  6.17 us
    ppermute x1, starting transfers between devices, local(): other = lax.ppermute(mine, 'core', [(0, 1), (1, 0)])  5.45 us
  transfers between devices with their start and end apart: 1, of which 1 were waited for; matrix products, arithmetic and copies ran while one was open for 0% of the time, Pallas kernels for 1%

profile of v5, /device:TPU:1, one launch (start us, length us, event | category | flops | bytes accessed | tf_op | source)
XLA Modules:
  0.0 88.9 jit_solution(16180378085565787173)
XLA Ops:
  0.7 1.0 %broadcast_select_fusion.pair_ref = f32[2,144,128]{2,1,0:T(8,128)S(1)} fusion(f32[144,128]{1,0:T(8,128)} %bitcast.15, f32[144,128]{1,0:T(8,128)} %bitcast.16, pred[2]{0:T(512)(128)(4,1)S(1)} %iota_compare_fusion), kind=kLoop, calls=%fused_computation | loop fusion | flops 36864 | bytes 294914 | tf_op jit(solution)/shard_map/jit(_where)/select_n | solution.py:280
  1.7 0.7 sums.1
  2.4 20.0 %all_to_all.20 = f32[16,1,128]{2,1,0:T(1,128)S(1)} all-to-all(f32[16,1,128]{2,1,0:T(1,128)S(1)} %bitcast.13), channel_id=1, replica_groups=mesh['x'=4,'y'=8,'core'=2,'group'=12] {'y','core'}, dimensions={0} | all-to-all | bytes 16384 | tf_op jit(solution)/shard_map/all_to_all | solution.py:282
  22.4 0.2 combine.1
  22.5 24.4 %all_to_all.21 = f32[48,1,128]{2,1,0:T(1,128)S(1)} all-to-all(f32[48,1,128]{2,1,0:T(1,128)S(1)} %bitcast.11), channel_id=1, replica_groups=mesh['x'=4,'y'=8,'core'=2,'group'=12] {'x','group'}, dimensions={0} | all-to-all | bytes 49152 | tf_op jit(solution)/shard_map/all_to_all | solution.py:284
  46.9 0.3 scale.1
  47.2 14.5 %all_to_all.22.in_ref = bf16[8,144,128]{2,1,0:T(8,128)(2,1)S(1)} all-to-all(bf16[8,144,128]{2,1,0:T(8,128)(2,1)S(1)} %get-tuple-element.13), channel_id=1, replica_groups={{0,48,96,144,192,240,288,336},{24,72,120,168,216,264,312,360},{384,432,..., dimensions={0} | all-to-all | bytes 589824 | tf_op jit(solution)/shard_map/all_to_all | solution.py:291
  61.7 0.3 turn.1
  62.0 12.9 %all_to_all.23.mine_ref = bf16[4,576,256]{2,1,0:T(8,128)(2,1)S(1)} all-to-all(bf16[4,576,256]{2,1,0:T(8,128)(2,1)S(1)} %turn.1), channel_id=1, replica_groups={{192,216,384,408},{240,264,432,456},{288,312,480,504},{336,360,528,552}..., dimensions={0} | all-to-all | bytes 2359296 | tf_op jit(solution)/shard_map/all_to_all | solution.py:299
  74.9 5.5 %collective-permute-start = (bf16[4,576,256]{2,1,0:T(8,128)(2,1)S(1)}, bf16[4,576,256]{2,1,0:T(8,128)(2,1)S(1)}, u32[]{:S(2)}, u32[]{:S(2)}) collective-permute-start(bf16[4,576,256]{2,1,0:T(8,128)(2,1)S(1)} %all_to_all.23.mine_ref), channel_id=1, source_target_pairs={{0,12},{12,0},{1,13},{13,1},{2,14},{14,2},{3,15},{15,3},{4,16},{16... | collective-permute-start | bytes 3538952 | tf_op jit(solution)/shard_map/ppermute | solution.py:300
  80.3 1.3 %gram.1 = (f32[576,576]{1,0:T(8,128)S(1)}, f32[1,144,128]{2,1,0:T(8,128)}) custom-call(bf16[4,576,256]{2,1,0:T(8,128)(2,1)S(1)} %all_to_all.23.mine_ref, f32[2,144,128]{2,1,0:T(8,128)S(1)} %broadcast_select_fusion.pair_ref, f32[8,128]{1,0:T(8,128)S(1)} %get-tuple-element.14.scale_ref), custom_call_target="tpu_custom_call" | custom-call | flops 679477248 | bytes 1179648 | tf_op jit(solution)/shard_map/gram/pallas_call | solution.py:301
  81.6 1.2 %collective-permute-done.other_ref = bf16[4,576,256]{2,1,0:T(8,128)(2,1)S(1)} collective-permute-done((bf16[4,576,256]{2,1,0:T(8,128)(2,1)S(1)}, bf16[4,576,256]{2,1,0:T(8,128)(2,1)S(1)}, u32[]{:S(2)}, u32[]{:S(2)}) %collective-permute-start) | collective-permute-done | bytes 1179680 | tf_op jit(solution)/shard_map/ppermute | solution.py:300
  82.8 6.2 %newton.1 = bf16[1,144,128]{2,1,0:T(8,128)(2,1)} custom-call(bf16[4,576,256]{2,1,0:T(8,128)(2,1)S(1)} %all_to_all.23.mine_ref, bf16[4,576,256]{2,1,0:T(8,128)(2,1)S(1)} %collective-permute-done.other_ref, f32[576,576]{1,0:T(8,128)S(1)} %get-tuple-element.16.gram_ref, f32[144,128]{1,0:T(8,128)S(1)} %get-tuple-element.17.own_ref), custom_call_target="tpu_custom_call" | custom-call | tf_op jit(solution)/shard_map/newton/pallas_call | solution.py:308
  (1 shorter events, 0.0 us)
Async XLA Ops:
  74.9 7.9 %collective-permute-start = (bf16[4,576,256]{2,1,0:T(8,128)(2,1)S(1)}, bf16[4,576,256]{2,1,0:T(8,128)(2,1)S(1)}, u32[]{:S(2)}, u32[]{:S(2)}) collective-permute-start(bf16[4,576,256]{2,1,0:T(8,128)(2,1)S(1)} %all_to_all.23.mine_ref), channel_id=1, source_target_pairs={{0,12},{12,0},{1,13},{13,1},{2,14},{14,2},{3,15},{15,3},{4,16},{16... | collective-permute-start | bytes 3538952 | tf_op jit(solution)/shard_map/ppermute | solution.py:300

commit v6 on v5

--- a/solution.py
+++ b/solution.py
@@ -63,16 +63,21 @@
     return float(high), float(np.float32(value - float(high)))
 
 
+def lazy_add(a, b):
+    s, e = two_sum(a[0], b[0])
+    return s, (a[1] + b[1]) + e
+
+
 def tree(values):
     while len(values) > 1:
-        paired = [dd_add(values[i], values[i + 1]) for i in range(0, len(values) - 1, 2)]
+        paired = [lazy_add(values[i], values[i + 1]) for i in range(0, len(values) - 1, 2)]
         values = paired + ([values[-1]] if len(values) % 2 else [])
     return values[0]
 
 
 def fold(a, axis, shifts):
     for shift in shifts:
-        a = dd_add(a, (pltpu.roll(a[0], shift, axis), pltpu.roll(a[1], shift, axis)))
+        a = lazy_add(a, (pltpu.roll(a[0], shift, axis), pltpu.roll(a[1], shift, axis)))
     return a
 
 
@@ -94,7 +99,7 @@
     return fast_two_sum(high, low + pltpu.roll(high, 64, 1))
 
 
-def sums_kernel(pair_ref, out_ref):
+def sums_kernel(groups, group_ref, pair_ref, out_ref):
     gg, gm, mm = [], [], []
     for i in range(0, pair_ref.shape[1], 8):
         g = pair_ref[0, i : i + 8, :]
@@ -103,19 +108,18 @@
         gm.append(two_prod(g, m))
         mm.append(two_prod(m, m))
     sums = [fold(fold(tree(v), 0, (4, 2, 1)), 1, (64, 32, 16, 8, 4, 2, 1)) for v in (gg, gm, mm)]
-    tile = pack([sums[0]] + sums)
+    tile = pack([fast_two_sum(*v) for v in [sums[0]] + sums])
+    for i in range(0, out_ref.shape[0], 8):
+        to = lax.rem(lax.broadcasted_iota(jnp.int32, (8, 128), 0) + i, groups)
+        keep = (to == group_ref[0]) | (lax.rem(lanes(), 64) == 0)
+        out_ref[i : i + 8, :] = jnp.where(keep, tile, 0.0)
+
+
+def combine_kernel(in_ref, out_ref):
+    high, low = add_rows(in_ref)
+    tile = jnp.where(lanes() < 64, high, pltpu.roll(low, 64, 1))
     for i in range(0, out_ref.shape[0], 8):
         out_ref[i : i + 8, :] = tile
-
-
-def combine_kernel(groups, group_ref, in_ref, out_ref):
-    high, low = add_rows(in_ref)
-    lane = lanes()
-    tile = jnp.where(lane < 64, high, pltpu.roll(low, 64, 1))
-    for i in range(0, out_ref.shape[0], 8):
-        to = lax.rem(lax.broadcasted_iota(jnp.int32, (8, 128), 0) + i, groups)
-        keep = (to == group_ref[0]) | (lax.rem(lane, 64) == 0)
-        out_ref[i : i + 8, :] = jnp.where(keep, tile, 0.0)
 
 
 def scale_kernel(entries, in_ref, pair_ref, out_ref, own_ref, scale_ref):
@@ -278,10 +282,10 @@
     grad, momentum, group = lax.optimization_barrier((grad, momentum, group))
     first = lax.broadcasted_iota(jnp.int32, (2, rows, 128), 0) == 0
     pair = jnp.where(first, grad, momentum)
-    sums = kernel(sums_kernel, "sums", shape((ny * nc, 128), f32), [VMEM])(pair)
+    sums = kernel(functools.partial(sums_kernel, ng), "sums", shape((nx * ng, 128), f32), [SMEM, VMEM])(group, pair)
+    sums = lax.all_to_all(sums.reshape(-1, 1, 128), ("x", "group"), 0, 0).reshape(-1, 128)
+    sums = kernel(combine_kernel, "combine", shape((ny * nc, 128), f32), [VMEM])(sums)
     sums = lax.all_to_all(sums.reshape(-1, 1, 128), ("y", "core"), 0, 0).reshape(-1, 128)
-    sums = kernel(functools.partial(combine_kernel, ng), "combine", shape((nx * ng, 128), f32), [SMEM, VMEM])(group, sums)
-    sums = lax.all_to_all(sums.reshape(-1, 1, 128), ("x", "group"), 0, 0).reshape(-1, 128)
     iterate, own, scale = kernel(
         functools.partial(scale_kernel, entries),
         "scale",

time: 89.3 us -> 90 us (level)
  blocking collectives: 71.7 us -> 74.6 us
  starting transfers between devices: 5.45 us -> 3.43 us
    all_to_all x1, blocking collectives: 24.4 us -> 29.8 us  [local(): lax.all_to_all(sums.reshape(-1, 1, 128), ('x', 'group'), 0, 0)]
    all_to_all x1, blocking collectives: 20 us -> 16 us  [local(): lax.all_to_all(sums.reshape(-1, 1, 128), ('y', 'core'), 0, 0)]
    ppermute x1, starting transfers between devices: 5.45 us -> 3.43 us  [local(): other = lax.ppermute(mine, 'core', [(0, 1), (1, 0)])]
    all_to_all x1, blocking collectives: 14.5 us -> 16.2 us  [local(): lax.all_to_all(iterate, chips, 0, 0, axis_index_groups=first_groups)]
where the time goes in v6:
time: 90 us; the launch traced here: 89.7 us
  blocking collectives  74.6 us (83%)
  Pallas kernels  8.78 us (10%)
  starting transfers between devices  3.43 us (4%)
  waiting for transfers between devices  1.17 us (1%)
  other arithmetic  1.01 us (1%)
    all_to_all x1, blocking collectives, local(): lax.all_to_all(sums.reshape(-1, 1, 128), ('x', 'group'), 0, 0)  29.8 us
    all_to_all x1, blocking collectives, local(): lax.all_to_all(iterate, chips, 0, 0, axis_index_groups=first_groups)  16.2 us
    all_to_all x1, blocking collectives, local(): lax.all_to_all(sums.reshape(-1, 1, 128), ('y', 'core'), 0, 0)  16 us
    all_to_all x1, blocking collectives, local(): mine = lax.all_to_all(turned, chips, 0, 0, axis_index_groups=second_groups)  12.7 us
    pallas_call x1, Pallas kernels, local(): kernel(functools.partial(iterate_kernel, update_scale), 'newton', shape(g...  6.17 us
    ppermute x1, starting transfers between devices, local(): other = lax.ppermute(mine, 'core', [(0, 1), (1, 0)])  3.43 us
  transfers between devices with their start and end apart: 1, of which 1 were waited for; matrix products, arithmetic and copies ran while one was open for 0% of the time, Pallas kernels for 1%

profile of v6, /device:TPU:1, one launch (start us, length us, event | category | flops | bytes accessed | tf_op | source)
XLA Modules:
  0.0 89.7 jit_solution(9086933900568640941)
XLA Ops:
  0.7 1.0 %broadcast_select_fusion.pair_ref = f32[2,144,128]{2,1,0:T(8,128)S(1)} fusion(f32[144,128]{1,0:T(8,128)} %bitcast.15, f32[144,128]{1,0:T(8,128)} %bitcast.16, pred[2]{0:T(512)(128)(4,1)S(1)} %iota_compare_fusion), kind=kLoop, calls=%fused_computation | loop fusion | flops 36864 | bytes 294914 | tf_op jit(solution)/shard_map/jit(_where)/select_n | solution.py:284
  1.7 0.7 sums.1
  2.3 29.8 %all_to_all.20 = f32[48,1,128]{2,1,0:T(1,128)S(1)} all-to-all(f32[48,1,128]{2,1,0:T(1,128)S(1)} %bitcast.12), channel_id=1, replica_groups=mesh['x'=4,'y'=8,'core'=2,'group'=12] {'x','group'}, dimensions={0} | all-to-all | bytes 49152 | tf_op jit(solution)/shard_map/all_to_all | solution.py:286
  32.1 0.2 combine.1
  32.2 16.0 %all_to_all.21 = f32[16,1,128]{2,1,0:T(1,128)S(1)} all-to-all(f32[16,1,128]{2,1,0:T(1,128)S(1)} %bitcast.14), channel_id=1, replica_groups=mesh['x'=4,'y'=8,'core'=2,'group'=12] {'y','core'}, dimensions={0} | all-to-all | bytes 16384 | tf_op jit(solution)/shard_map/all_to_all | solution.py:288
  48.2 0.3 scale.1
  48.5 16.2 %all_to_all.22.in_ref = bf16[8,144,128]{2,1,0:T(8,128)(2,1)S(1)} all-to-all(bf16[8,144,128]{2,1,0:T(8,128)(2,1)S(1)} %get-tuple-element.13), channel_id=1, replica_groups={{0,48,96,144,192,240,288,336},{24,72,120,168,216,264,312,360},{384,432,..., dimensions={0} | all-to-all | bytes 589824 | tf_op jit(solution)/shard_map/all_to_all | solution.py:295
  64.7 0.3 turn.1
  64.9 12.7 %all_to_all.23.mine_ref = bf16[4,576,256]{2,1,0:T(8,128)(2,1)S(1)} all-to-all(bf16[4,576,256]{2,1,0:T(8,128)(2,1)S(1)} %turn.1), channel_id=1, replica_groups={{192,216,384,408},{240,264,432,456},{288,312,480,504},{336,360,528,552}..., dimensions={0} | all-to-all | bytes 2359296 | tf_op jit(solution)/shard_map/all_to_all | solution.py:303
  77.6 3.4 %collective-permute-start = (bf16[4,576,256]{2,1,0:T(8,128)(2,1)S(1)}, bf16[4,576,256]{2,1,0:T(8,128)(2,1)S(1)}, u32[]{:S(2)}, u32[]{:S(2)}) collective-permute-start(bf16[4,576,256]{2,1,0:T(8,128)(2,1)S(1)} %all_to_all.23.mine_ref), channel_id=1, source_target_pairs={{0,12},{12,0},{1,13},{13,1},{2,14},{14,2},{3,15},{15,3},{4,16},{16... | collective-permute-start | bytes 3538952 | tf_op jit(solution)/shard_map/ppermute | solution.py:304
  81.1 1.3 %gram.1 = (f32[576,576]{1,0:T(8,128)S(1)}, f32[1,144,128]{2,1,0:T(8,128)}) custom-call(bf16[4,576,256]{2,1,0:T(8,128)(2,1)S(1)} %all_to_all.23.mine_ref, f32[2,144,128]{2,1,0:T(8,128)S(1)} %broadcast_select_fusion.pair_ref, f32[8,128]{1,0:T(8,128)S(1)} %get-tuple-element.14.scale_ref), custom_call_target="tpu_custom_call" | custom-call | flops 679477248 | bytes 1179648 | tf_op jit(solution)/shard_map/gram/pallas_call | solution.py:305
  82.4 1.2 %collective-permute-done.other_ref = bf16[4,576,256]{2,1,0:T(8,128)(2,1)S(1)} collective-permute-done((bf16[4,576,256]{2,1,0:T(8,128)(2,1)S(1)}, bf16[4,576,256]{2,1,0:T(8,128)(2,1)S(1)}, u32[]{:S(2)}, u32[]{:S(2)}) %collective-permute-start) | collective-permute-done | bytes 1179680 | tf_op jit(solution)/shard_map/ppermute | solution.py:304
  83.5 6.2 %newton.1 = bf16[1,144,128]{2,1,0:T(8,128)(2,1)} custom-call(bf16[4,576,256]{2,1,0:T(8,128)(2,1)S(1)} %all_to_all.23.mine_ref, bf16[4,576,256]{2,1,0:T(8,128)(2,1)S(1)} %collective-permute-done.other_ref, f32[576,576]{1,0:T(8,128)S(1)} %get-tuple-element.16.gram_ref, f32[144,128]{1,0:T(8,128)S(1)} %get-tuple-element.17.own_ref), custom_call_target="tpu_custom_call" | custom-call | tf_op jit(solution)/shard_map/newton/pallas_call | solution.py:312
  (1 shorter events, 0.0 us)
Async XLA Ops:
  77.6 5.9 %collective-permute-start = (bf16[4,576,256]{2,1,0:T(8,128)(2,1)S(1)}, bf16[4,576,256]{2,1,0:T(8,128)(2,1)S(1)}, u32[]{:S(2)}, u32[]{:S(2)}) collective-permute-start(bf16[4,576,256]{2,1,0:T(8,128)(2,1)S(1)} %all_to_all.23.mine_ref), channel_id=1, source_target_pairs={{0,12},{12,0},{1,13},{13,1},{2,14},{14,2},{3,15},{15,3},{4,16},{16... | collective-permute-start | bytes 3538952 | tf_op jit(solution)/shard_map/ppermute | solution.py:304

commit v7 on v5

--- a/solution.py
+++ b/solution.py
@@ -63,16 +63,21 @@
     return float(high), float(np.float32(value - float(high)))
 
 
+def lazy_add(a, b):
+    s, e = two_sum(a[0], b[0])
+    return s, (a[1] + b[1]) + e
+
+
 def tree(values):
     while len(values) > 1:
-        paired = [dd_add(values[i], values[i + 1]) for i in range(0, len(values) - 1, 2)]
+        paired = [lazy_add(values[i], values[i + 1]) for i in range(0, len(values) - 1, 2)]
         values = paired + ([values[-1]] if len(values) % 2 else [])
     return values[0]
 
 
 def fold(a, axis, shifts):
     for shift in shifts:
-        a = dd_add(a, (pltpu.roll(a[0], shift, axis), pltpu.roll(a[1], shift, axis)))
+        a = lazy_add(a, (pltpu.roll(a[0], shift, axis), pltpu.roll(a[1], shift, axis)))
     return a
 
 
@@ -103,7 +108,7 @@
         gm.append(two_prod(g, m))
         mm.append(two_prod(m, m))
     sums = [fold(fold(tree(v), 0, (4, 2, 1)), 1, (64, 32, 16, 8, 4, 2, 1)) for v in (gg, gm, mm)]
-    tile = pack([sums[0]] + sums)
+    tile = pack([fast_two_sum(*v) for v in [sums[0]] + sums])
     for i in range(0, out_ref.shape[0], 8):
         out_ref[i : i + 8, :] = tile
 
@@ -225,11 +230,12 @@
         v = r[k]
         product = jnp.dot(poly_ref[...], v, preferred_element_type=f32)
         next_ref[i] = (coef_first * v.astype(f32) + product).astype(bf16)
+    columns = gram_columns(side_by_side([next_ref[i] for i in range(len(blocks))]))
     own = own_load(own_ref, pairs)
     product = jnp.dot(own.astype(bf16), poly_ref[...], preferred_element_type=f32)
     own = (coef_first * own + product).astype(bf16)
-    store_poly(gram_columns(side_by_side([next_ref[i] for i in range(len(blocks))])), low_ref, poly_ref)
-    product = jnp.dot(own, poly_ref[...], preferred_element_type=f32)
+    store_poly(columns, low_ref, poly_ref)
+    product = side_by_side([jnp.dot(own, poly_ref[:, a:b], preferred_element_type=f32) for a, b in triangle()])
     own_store(flat_ref, update_scale * (coef_first * own.astype(f32) + product), pairs)
     out_ref[0] = flat_ref[...].astype(bf16)
 

time: 89.3 us -> 88.9 us (level)
  no operation moved by 1% of the time
where the time goes in v7:
time: 88.9 us; the launch traced here: 88.6 us
  blocking collectives  71.7 us (81%)
  Pallas kernels  8.59 us (10%)
  starting transfers between devices  5.45 us (6%)
  waiting for transfers between devices  1.17 us (1%)
  other arithmetic  1.01 us (1%)
    all_to_all x1, blocking collectives, local(): lax.all_to_all(sums.reshape(-1, 1, 128), ('x', 'group'), 0, 0)  24.4 us
    all_to_all x1, blocking collectives, local(): lax.all_to_all(sums.reshape(-1, 1, 128), ('y', 'core'), 0, 0)  20 us
    all_to_all x1, blocking collectives, local(): lax.all_to_all(iterate, chips, 0, 0, axis_index_groups=first_groups)  14.5 us
    all_to_all x1, blocking collectives, local(): mine = lax.all_to_all(turned, chips, 0, 0, axis_index_groups=second_groups)  12.9 us
    pallas_call x1, Pallas kernels, local(): kernel(functools.partial(iterate_kernel, update_scale), 'newton', shape(g...  5.99 us
    ppermute x1, starting transfers between devices, local(): other = lax.ppermute(mine, 'core', [(0, 1), (1, 0)])  5.45 us
  transfers between devices with their start and end apart: 1, of which 1 were waited for; matrix products, arithmetic and copies ran while one was open for 0% of the time, Pallas kernels for 1%

profile of v7, /device:TPU:1, one launch (start us, length us, event | category | flops | bytes accessed | tf_op | source)
XLA Modules:
  0.0 88.6 jit_solution(15363644925714349091)
XLA Ops:
  0.7 1.0 %broadcast_select_fusion.pair_ref = f32[2,144,128]{2,1,0:T(8,128)S(1)} fusion(f32[144,128]{1,0:T(8,128)} %bitcast.15, f32[144,128]{1,0:T(8,128)} %bitcast.16, pred[2]{0:T(512)(128)(4,1)S(1)} %iota_compare_fusion), kind=kLoop, calls=%fused_computation | loop fusion | flops 36864 | bytes 294914 | tf_op jit(solution)/shard_map/jit(_where)/select_n | solution.py:286
  1.7 0.7 sums.1
  2.3 20.0 %all_to_all.20 = f32[16,1,128]{2,1,0:T(1,128)S(1)} all-to-all(f32[16,1,128]{2,1,0:T(1,128)S(1)} %bitcast.13), channel_id=1, replica_groups=mesh['x'=4,'y'=8,'core'=2,'group'=12] {'y','core'}, dimensions={0} | all-to-all | bytes 16384 | tf_op jit(solution)/shard_map/all_to_all | solution.py:288
  22.3 0.2 combine.1
  22.4 24.4 %all_to_all.21 = f32[48,1,128]{2,1,0:T(1,128)S(1)} all-to-all(f32[48,1,128]{2,1,0:T(1,128)S(1)} %bitcast.11), channel_id=1, replica_groups=mesh['x'=4,'y'=8,'core'=2,'group'=12] {'x','group'}, dimensions={0} | all-to-all | bytes 49152 | tf_op jit(solution)/shard_map/all_to_all | solution.py:290
  46.8 0.3 scale.1
  47.1 14.5 %all_to_all.22.in_ref = bf16[8,144,128]{2,1,0:T(8,128)(2,1)S(1)} all-to-all(bf16[8,144,128]{2,1,0:T(8,128)(2,1)S(1)} %get-tuple-element.13), channel_id=1, replica_groups={{0,48,96,144,192,240,288,336},{24,72,120,168,216,264,312,360},{384,432,..., dimensions={0} | all-to-all | bytes 589824 | tf_op jit(solution)/shard_map/all_to_all | solution.py:297
  61.5 0.3 turn.1
  61.8 12.9 %all_to_all.23.mine_ref = bf16[4,576,256]{2,1,0:T(8,128)(2,1)S(1)} all-to-all(bf16[4,576,256]{2,1,0:T(8,128)(2,1)S(1)} %turn.1), channel_id=1, replica_groups={{192,216,384,408},{240,264,432,456},{288,312,480,504},{336,360,528,552}..., dimensions={0} | all-to-all | bytes 2359296 | tf_op jit(solution)/shard_map/all_to_all | solution.py:305
  74.7 5.5 %collective-permute-start = (bf16[4,576,256]{2,1,0:T(8,128)(2,1)S(1)}, bf16[4,576,256]{2,1,0:T(8,128)(2,1)S(1)}, u32[]{:S(2)}, u32[]{:S(2)}) collective-permute-start(bf16[4,576,256]{2,1,0:T(8,128)(2,1)S(1)} %all_to_all.23.mine_ref), channel_id=1, source_target_pairs={{0,12},{12,0},{1,13},{13,1},{2,14},{14,2},{3,15},{15,3},{4,16},{16... | collective-permute-start | bytes 3538952 | tf_op jit(solution)/shard_map/ppermute | solution.py:306
  80.2 1.3 %gram.1 = (f32[576,576]{1,0:T(8,128)S(1)}, f32[1,144,128]{2,1,0:T(8,128)}) custom-call(bf16[4,576,256]{2,1,0:T(8,128)(2,1)S(1)} %all_to_all.23.mine_ref, f32[2,144,128]{2,1,0:T(8,128)S(1)} %broadcast_select_fusion.pair_ref, f32[8,128]{1,0:T(8,128)S(1)} %get-tuple-element.14.scale_ref), custom_call_target="tpu_custom_call" | custom-call | flops 679477248 | bytes 1179648 | tf_op jit(solution)/shard_map/gram/pallas_call | solution.py:307
  81.5 1.2 %collective-permute-done.other_ref = bf16[4,576,256]{2,1,0:T(8,128)(2,1)S(1)} collective-permute-done((bf16[4,576,256]{2,1,0:T(8,128)(2,1)S(1)}, bf16[4,576,256]{2,1,0:T(8,128)(2,1)S(1)}, u32[]{:S(2)}, u32[]{:S(2)}) %collective-permute-start) | collective-permute-done | bytes 1179680 | tf_op jit(solution)/shard_map/ppermute | solution.py:306
  82.6 6.0 %newton.1 = bf16[1,144,128]{2,1,0:T(8,128)(2,1)} custom-call(bf16[4,576,256]{2,1,0:T(8,128)(2,1)S(1)} %all_to_all.23.mine_ref, bf16[4,576,256]{2,1,0:T(8,128)(2,1)S(1)} %collective-permute-done.other_ref, f32[576,576]{1,0:T(8,128)S(1)} %get-tuple-element.16.gram_ref, f32[144,128]{1,0:T(8,128)S(1)} %get-tuple-element.17.own_ref), custom_call_target="tpu_custom_call" | custom-call | tf_op jit(solution)/shard_map/newton/pallas_call | solution.py:314
  (1 shorter events, 0.0 us)
Async XLA Ops:
  74.7 7.9 %collective-permute-start = (bf16[4,576,256]{2,1,0:T(8,128)(2,1)S(1)}, bf16[4,576,256]{2,1,0:T(8,128)(2,1)S(1)}, u32[]{:S(2)}, u32[]{:S(2)}) collective-permute-start(bf16[4,576,256]{2,1,0:T(8,128)(2,1)S(1)} %all_to_all.23.mine_ref), channel_id=1, source_target_pairs={{0,12},{12,0},{1,13},{13,1},{2,14},{14,2},{3,15},{15,3},{4,16},{16... | collective-permute-start | bytes 3538952 | tf_op jit(solution)/shard_map/ppermute | solution.py:306

commit v8 on v7

--- a/solution.py
+++ b/solution.py
@@ -213,24 +213,33 @@
         mirror(poly_ref, (coef_second * column + coef_third * squared).astype(bf16), a, b)
 
 
-def gram_kernel(mine_ref, pair_ref, scale_ref, gram_ref, momentum_out_ref):
-    iterate = side_by_side([mine_ref[i] for i in range(mine_ref.shape[0])])
-    for (a, b), column in zip(triangle(), gram_columns(iterate)):
+def joined(ref):
+    return side_by_side([ref[i] for i in range(ref.shape[0])])
+
+
+def gram_kernel(block_ref, pair_ref, scale_ref, gram_ref, momentum_out_ref):
+    for (a, b), column in zip(triangle(), gram_columns(joined(block_ref))):
         gram_ref[a:, a:b] = column
     momentum_out_ref[0] = momentum_rate * pair_ref[1] + scale_ref[0:1, :] * pair_ref[0]
 
 
-def iterate_kernel(update_scale, mine_ref, other_ref, gram_ref, own_ref, out_ref, poly_ref, next_ref, flat_ref, low_ref):
-    blocks = [(r, i) for r in (mine_ref, other_ref) for i in range(r.shape[0])]
+def more_gram_kernel(block_ref, gram_ref, out_ref):
+    for (a, b), column in zip(triangle(), gram_columns(joined(block_ref))):
+        out_ref[a:, a:b] = gram_ref[a:, a:b] + column
+
+
+def iterate_kernel(update_scale, parts, *refs):
+    block_refs = refs[:parts]
+    gram_ref, own_ref, out_ref, poly_ref, next_ref, flat_ref, low_ref = refs[parts:]
+    blocks = [side_by_side([r[i], r[i + 1]]) for r in block_refs for i in range(0, r.shape[0], 2)]
     pairs = own_ref.shape[0] // 9
-    columns = gram_columns(side_by_side([other_ref[i] for i in range(other_ref.shape[0])]))
+    columns = gram_columns(joined(block_refs[-1]))
     columns = [gram_ref[a:, a:b] + column for (a, b), column in zip(triangle(), columns)]
     store_poly(columns, low_ref, poly_ref)
-    for i, (r, k) in enumerate(blocks):
-        v = r[k]
+    for i, v in enumerate(blocks):
         product = jnp.dot(poly_ref[...], v, preferred_element_type=f32)
         next_ref[i] = (coef_first * v.astype(f32) + product).astype(bf16)
-    columns = gram_columns(side_by_side([next_ref[i] for i in range(len(blocks))]))
+    columns = gram_columns(joined(next_ref))
     own = own_load(own_ref, pairs)
     product = jnp.dot(own.astype(bf16), poly_ref[...], preferred_element_type=f32)
     own = (coef_first * own + product).astype(bf16)
@@ -248,15 +257,17 @@
     def at(x, y, core):
         return (x * ny + y) * nc + core
 
-    first, second = [], []
+    first, second, swap, cores = [], [], [], []
     for core in range(nc):
+        for x in range(nx):
+            first += [[at(x, y, core) for y in range(parity, ny, 2)] for parity in range(2)]
+            cores += [(at(x, y, core), at(x, y, 1 - core)) for y in range(ny)]
         for xs in pairings(nx, core):
-            for parity in range(2):
-                first.append([at(x, y, core) for x in xs for y in range(parity, ny, 2)])
-        for xs in pairings(nx, 1 - core):
-            for ys in pairings(ny, core):
-                second.append([at(x, y, core) for x in xs for y in ys])
-    return first, second
+            second += [[at(x, y, core) for x in xs for y in ys] for ys in pairings(ny, core)]
+        for x, other in pairings(nx, 1 - core):
+            for y in range(ny):
+                swap += [(at(x, y, core), at(other, y, core)), (at(other, y, core), at(x, y, core))]
+    return first, second, swap, cores
 
 
 def kernel(body, name, out, in_specs, scratch=(), cost=None):
@@ -275,7 +286,7 @@
 def local(entries, update_scale, sizes, grad, momentum):
     nx, ny, nc, ng = sizes
     chips = ("x", "y", "core")
-    first_groups, second_groups = gather_groups(nx, ny, nc)
+    first_groups, second_groups, swap, cores = gather_groups(nx, ny, nc)
     blocks, copies = len(first_groups[0]), len(second_groups[0])
     rows = grad.shape[1]
     columns = blocks * rows * 128 // ROWS
@@ -303,26 +314,28 @@
         scratch=[pltpu.VMEM((blocks * rows, 128), f32)],
     )(gathered)
     mine = lax.all_to_all(turned, chips, 0, 0, axis_index_groups=second_groups)
-    other = lax.ppermute(mine, "core", [(0, 1), (1, 0)])
-    gram, momentum_out = kernel(
-        gram_kernel,
-        "gram",
-        (shape((ROWS, ROWS), f32), shape(grad.shape, f32)),
-        [VMEM] * 3,
-        cost=pl.CostEstimate(flops=2 * ROWS * ROWS * columns * copies, bytes_accessed=2 * ROWS * columns * copies, transcendentals=0),
-    )(mine, pair, scale)
+    far = lax.ppermute(mine, chips, swap)
+    other = lax.ppermute(mine, chips, cores)
+    cost = pl.CostEstimate(flops=2 * ROWS * ROWS * columns * copies, bytes_accessed=2 * ROWS * columns * copies, transcendentals=0)
+    gram_shape = shape((ROWS, ROWS), f32)
+    gram, momentum_out = kernel(gram_kernel, "gram", (gram_shape, shape(grad.shape, f32)), [VMEM] * 3, cost=cost)(mine, pair, scale)
+    gram = kernel(more_gram_kernel, "gram_other", gram_shape, [VMEM] * 2, cost=cost)(other, gram)
+    far, gram = lax.optimization_barrier((far, gram))
+    far_other = lax.ppermute(far, chips, cores)
+    gram = kernel(more_gram_kernel, "gram_far", gram_shape, [VMEM] * 2, cost=cost)(far, gram)
+    parts = (mine, other, far, far_other)
     update = kernel(
-        functools.partial(iterate_kernel, update_scale),
+        functools.partial(iterate_kernel, update_scale, len(parts)),
         "newton",
         shape(grad.shape, bf16),
-        [VMEM] * 4,
+        [VMEM] * (len(parts) + 2),
         scratch=[
             pltpu.VMEM((ROWS, ROWS), bf16),
-            pltpu.VMEM((2 * copies, ROWS, columns), bf16),
+            pltpu.VMEM((len(parts) * copies // 2, ROWS, 2 * columns), bf16),
             pltpu.VMEM((rows, 128), f32),
             pltpu.VMEM((ROWS, ROWS), bf16),
         ],
-    )(mine, other, gram, own)
+    )(*parts, gram, own)
     return momentum_out, update
 
 

time: 88.9 us -> 94.8 us (1.066)
  waiting for transfers between devices: 1.17 us -> 8.19 us
  blocking collectives: 71.7 us -> 64.8 us
  starting transfers between devices: 5.45 us -> 10.8 us
    ppermute x1 -> x3, waiting for transfers between devices: 1.17 us -> 8.19 us  [the longest x1 7.04 us: local(): far = lax.ppermute(mine, chips, swap)]
    ppermute x1 -> x3, starting transfers between devices: 5.45 us -> 10.8 us  [the longest x1 4.42 us: local(): other = lax.ppermute(mine, chips, cores)]
    all_to_all x1, blocking collectives: 14.5 us -> 9.84 us  [local(): lax.all_to_all(iterate, chips, 0, 0, axis_index_groups=first_groups)]
    all_to_all x1, blocking collectives: 12.9 us -> 10.6 us  [local(): mine = lax.all_to_all(turned, chips, 0, 0, axis_index_groups=second_groups)]
    pallas_call x2 -> x4, Pallas kernels: 7.27 us -> 7.64 us  [the longest x1 5.68 us: local(): kernel(functools.partial(iterate_kernel, update_scale, len(parts)), 'newt...]
  transfers between devices with their start and end apart: 1 -> 3, of which waited for: 1 -> 2; matrix products, arithmetic and copies ran while one was open for 0% -> 0% of each run, Pallas kernels for 1% -> 2%
where the time goes in v8:
time: 94.8 us; the launch traced here: 94.4 us
  blocking collectives  64.8 us (68%)
  starting transfers between devices  10.8 us (11%)
  Pallas kernels  9 us (9%)
  waiting for transfers between devices  8.19 us (9%)
  other arithmetic  1.01 us (1%)
    all_to_all x1, blocking collectives, local(): lax.all_to_all(sums.reshape(-1, 1, 128), ('x', 'group'), 0, 0)  24.4 us
    all_to_all x1, blocking collectives, local(): lax.all_to_all(sums.reshape(-1, 1, 128), ('y', 'core'), 0, 0)  20 us
    all_to_all x1, blocking collectives, local(): mine = lax.all_to_all(turned, chips, 0, 0, axis_index_groups=second_groups)  10.6 us
    all_to_all x1, blocking collectives, local(): lax.all_to_all(iterate, chips, 0, 0, axis_index_groups=first_groups)  9.84 us
    ppermute x1, waiting for transfers between devices, local(): far = lax.ppermute(mine, chips, swap)  7.04 us
    pallas_call x1, Pallas kernels, local(): kernel(functools.partial(iterate_kernel, update_scale, len(parts)), 'newt...  5.68 us
    ppermute x1, starting transfers between devices, local(): other = lax.ppermute(mine, chips, cores)  4.42 us
    ppermute x1, starting transfers between devices, local(): far_other = lax.ppermute(far, chips, cores)  3.97 us
  transfers between devices with their start and end apart: 3, of which 2 were waited for; matrix products, arithmetic and copies ran while one was open for 0% of the time, Pallas kernels for 2%

profile of v8, /device:TPU:1, one launch (start us, length us, event | category | flops | bytes accessed | tf_op | source)
XLA Modules:
  0.0 94.4 jit_solution(763583085938356912)
XLA Ops:
  0.7 1.0 %broadcast_select_fusion.pair_ref = f32[2,144,128]{2,1,0:T(8,128)S(1)} fusion(f32[144,128]{1,0:T(8,128)} %bitcast.15, f32[144,128]{1,0:T(8,128)} %bitcast.16, pred[2]{0:T(512)(128)(4,1)S(1)} %iota_compare_fusion), kind=kLoop, calls=%fused_computation | loop fusion | flops 36864 | bytes 294914 | tf_op jit(solution)/shard_map/jit(_where)/select_n | solution.py:297
  1.7 0.7 sums.1
  2.3 20.0 %all_to_all.20 = f32[16,1,128]{2,1,0:T(1,128)S(1)} all-to-all(f32[16,1,128]{2,1,0:T(1,128)S(1)} %bitcast.13), channel_id=1, replica_groups=mesh['x'=4,'y'=8,'core'=2,'group'=12] {'y','core'}, dimensions={0} | all-to-all | bytes 16384 | tf_op jit(solution)/shard_map/all_to_all | solution.py:299
  22.3 0.2 combine.1
  22.4 24.4 %all_to_all.21 = f32[48,1,128]{2,1,0:T(1,128)S(1)} all-to-all(f32[48,1,128]{2,1,0:T(1,128)S(1)} %bitcast.11), channel_id=1, replica_groups=mesh['x'=4,'y'=8,'core'=2,'group'=12] {'x','group'}, dimensions={0} | all-to-all | bytes 49152 | tf_op jit(solution)/shard_map/all_to_all | solution.py:301
  46.8 0.2 scale.1
  47.1 9.8 %all_to_all.22.in_ref = bf16[4,144,128]{2,1,0:T(8,128)(2,1)S(1)} all-to-all(bf16[4,144,128]{2,1,0:T(8,128)(2,1)S(1)} %get-tuple-element.15), channel_id=1, replica_groups={{0,48,96,144},{24,72,120,168},{192,240,288,336},{216,264,312,360},{384,..., dimensions={0} | all-to-all | bytes 294912 | tf_op jit(solution)/shard_map/all_to_all | solution.py:308
  56.9 0.3 turn.1
  57.2 10.6 %all_to_all.23.block_ref.refs_0_ = bf16[4,576,128]{2,1,0:T(8,128)(2,1)S(1)} all-to-all(bf16[4,576,128]{2,1,0:T(8,128)(2,1)S(1)} %turn.1), channel_id=1, replica_groups={{0,24,192,216},{48,72,240,264},{96,120,288,312},{144,168,336,360},{384,..., dimensions={0} | all-to-all | bytes 1179648 | tf_op jit(solution)/shard_map/all_to_all | solution.py:316
  67.8 4.4 %collective-permute-start = (bf16[4,576,128]{2,1,0:T(8,128)(2,1)S(1)}, bf16[4,576,128]{2,1,0:T(8,128)(2,1)S(1)}, u32[]{:S(2)}, u32[]{:S(2)}) collective-permute-start(bf16[4,576,128]{2,1,0:T(8,128)(2,1)S(1)} %all_to_all.23.block_ref.refs_0_), channel_id=1, source_target_pairs={{0,12},{24,36},{48,60},{72,84},{96,108},{120,132},{144,156},{168,1... | collective-permute-start | bytes 1769480 | tf_op jit(solution)/shard_map/ppermute | solution.py:318
  72.3 2.4 %collective-permute-start.1 = (bf16[4,576,128]{2,1,0:T(8,128)(2,1)S(1)}, bf16[4,576,128]{2,1,0:T(8,128)(2,1)S(1)}, u32[]{:S(2)}, u32[]{:S(2)}) collective-permute-start(bf16[4,576,128]{2,1,0:T(8,128)(2,1)S(1)} %all_to_all.23.block_ref.refs_0_), channel_id=1, source_target_pairs={{192,384},{384,192},{216,408},{408,216},{240,432},{432,240},{264,4... | collective-permute-start | bytes 1769480 | tf_op jit(solution)/shard_map/ppermute | solution.py:317
  74.6 1.0 %gram.1 = (f32[576,576]{1,0:T(8,128)S(1)}, f32[1,144,128]{2,1,0:T(8,128)}) custom-call(bf16[4,576,128]{2,1,0:T(8,128)(2,1)S(1)} %all_to_all.23.block_ref.refs_0_, f32[2,144,128]{2,1,0:T(8,128)S(1)} %broadcast_select_fusion.pair_ref, f32[8,128]{1,0:T(8,128)S(1)} %get-tuple-element.16.scale_ref), custom_call_target="tpu_custom_call" | custom-call | flops 339738624 | bytes 589824 | tf_op jit(solution)/shard_map/gram/pallas_call | solution.py:321
  75.7 0.0 collective-permute-done.block_ref.refs_1_
  75.7 0.5 gram_other.1.gram_ref
  76.1 7.0 %collective-permute-done.1.block_ref.refs_2_ = bf16[4,576,128]{2,1,0:T(8,128)(2,1)S(1)} collective-permute-done((bf16[4,576,128]{2,1,0:T(8,128)(2,1)S(1)}, bf16[4,576,128]{2,1,0:T(8,128)(2,1)S(1)}, u32[]{:S(2)}, u32[]{:S(2)}) %collective-permute-start.1) | collective-permute-done | bytes 589856 | tf_op jit(solution)/shard_map/ppermute | solution.py:317
  83.2 4.0 %collective-permute-start.2 = (bf16[4,576,128]{2,1,0:T(8,128)(2,1)S(1)}, bf16[4,576,128]{2,1,0:T(8,128)(2,1)S(1)}, u32[]{:S(2)}, u32[]{:S(2)}) collective-permute-start(bf16[4,576,128]{2,1,0:T(8,128)(2,1)S(1)} %collective-permute-done.1.block_ref.refs_2_), channel_id=1, source_target_pairs={{0,12},{24,36},{48,60},{72,84},{96,108},{120,132},{144,156},{168,1... | collective-permute-start | bytes 1769480 | tf_op jit(solution)/shard_map/ppermute | solution.py:324
  87.2 0.5 gram_far.1.refs_4_
  87.6 1.1 %collective-permute-done.2.refs_3_ = bf16[4,576,128]{2,1,0:T(8,128)(2,1)S(1)} collective-permute-done((bf16[4,576,128]{2,1,0:T(8,128)(2,1)S(1)}, bf16[4,576,128]{2,1,0:T(8,128)(2,1)S(1)}, u32[]{:S(2)}, u32[]{:S(2)}) %collective-permute-start.2) | collective-permute-done | bytes 589856 | tf_op jit(solution)/shard_map/ppermute | solution.py:324
  88.8 5.7 %newton.1 = bf16[1,144,128]{2,1,0:T(8,128)(2,1)} custom-call(bf16[4,576,128]{2,1,0:T(8,128)(2,1)S(1)} %all_to_all.23.block_ref.refs_0_, bf16[4,576,128]{2,1,0:T(8,128)(2,1)S(1)} %collective-permute-done.block_ref.refs_1_, bf16[4,576,128]{2,1,0:T(8,128)(2,1)S(1)} %collective-permute-done.1.block_ref.refs_2_, ...), custom_call_target="tpu_custom_call" | custom-call | tf_op jit(solution)/shard_map/newton/pallas_call | solution.py:327
  (1 shorter events, 0.0 us)
Async XLA Ops:
  67.8 7.8 %collective-permute-start = (bf16[4,576,128]{2,1,0:T(8,128)(2,1)S(1)}, bf16[4,576,128]{2,1,0:T(8,128)(2,1)S(1)}, u32[]{:S(2)}, u32[]{:S(2)}) collective-permute-start(bf16[4,576,128]{2,1,0:T(8,128)(2,1)S(1)} %all_to_all.23.block_ref.refs_0_), channel_id=1, source_target_pairs={{0,12},{24,36},{48,60},{72,84},{96,108},{120,132},{144,156},{168,1... | collective-permute-start | bytes 1769480 | tf_op jit(solution)/shard_map/ppermute | solution.py:318
  72.3 10.9 %collective-permute-start.1 = (bf16[4,576,128]{2,1,0:T(8,128)(2,1)S(1)}, bf16[4,576,128]{2,1,0:T(8,128)(2,1)S(1)}, u32[]{:S(2)}, u32[]{:S(2)}) collective-permute-start(bf16[4,576,128]{2,1,0:T(8,128)(2,1)S(1)} %all_to_all.23.block_ref.refs_0_), channel_id=1, source_target_pairs={{192,384},{384,192},{216,408},{408,216},{240,432},{432,240},{264,4... | collective-permute-start | bytes 1769480 | tf_op jit(solution)/shard_map/ppermute | solution.py:317
  83.2 5.6 %collective-permute-start.2 = (bf16[4,576,128]{2,1,0:T(8,128)(2,1)S(1)}, bf16[4,576,128]{2,1,0:T(8,128)(2,1)S(1)}, u32[]{:S(2)}, u32[]{:S(2)}) collective-permute-start(bf16[4,576,128]{2,1,0:T(8,128)(2,1)S(1)} %collective-permute-done.1.block_ref.refs_2_), channel_id=1, source_target_pairs={{0,12},{24,36},{48,60},{72,84},{96,108},{120,132},{144,156},{168,1... | collective-permute-start | bytes 1769480 | tf_op jit(solution)/shard_map/ppermute | solution.py:324

commit v9 on v7

--- a/solution.py
+++ b/solution.py
@@ -221,13 +221,12 @@
 
 
 def iterate_kernel(update_scale, mine_ref, other_ref, gram_ref, own_ref, out_ref, poly_ref, next_ref, flat_ref, low_ref):
-    blocks = [(r, i) for r in (mine_ref, other_ref) for i in range(r.shape[0])]
+    blocks = [side_by_side([r[i], r[i + 1]]) for r in (mine_ref, other_ref) for i in range(0, r.shape[0], 2)]
     pairs = own_ref.shape[0] // 9
     columns = gram_columns(side_by_side([other_ref[i] for i in range(other_ref.shape[0])]))
     columns = [gram_ref[a:, a:b] + column for (a, b), column in zip(triangle(), columns)]
     store_poly(columns, low_ref, poly_ref)
-    for i, (r, k) in enumerate(blocks):
-        v = r[k]
+    for i, v in enumerate(blocks):
         product = jnp.dot(poly_ref[...], v, preferred_element_type=f32)
         next_ref[i] = (coef_first * v.astype(f32) + product).astype(bf16)
     columns = gram_columns(side_by_side([next_ref[i] for i in range(len(blocks))]))
@@ -250,12 +249,9 @@
 
     first, second = [], []
     for core in range(nc):
-        for xs in pairings(nx, core):
-            for parity in range(2):
-                first.append([at(x, y, core) for x in xs for y in range(parity, ny, 2)])
-        for xs in pairings(nx, 1 - core):
-            for ys in pairings(ny, core):
-                second.append([at(x, y, core) for x in xs for y in ys])
+        for x in range(nx):
+            first += [[at(x, y, core) for y in range(parity, ny, 2)] for parity in range(2)]
+        second += [[at(x, y, core) for x in range(nx) for y in ys] for ys in pairings(ny, core)]
     return first, second
 
 
@@ -318,7 +314,7 @@
         [VMEM] * 4,
         scratch=[
             pltpu.VMEM((ROWS, ROWS), bf16),
-            pltpu.VMEM((2 * copies, ROWS, columns), bf16),
+            pltpu.VMEM((copies, ROWS, 2 * columns), bf16),
             pltpu.VMEM((rows, 128), f32),
             pltpu.VMEM((ROWS, ROWS), bf16),
         ],

time: 88.9 us -> 89.7 us (level)
  blocking collectives: 71.7 us -> 74.2 us
  starting transfers between devices: 5.45 us -> 3.51 us
    all_to_all x1, blocking collectives: 12.9 us -> 20 us  [local(): mine = lax.all_to_all(turned, chips, 0, 0, axis_index_groups=second_groups)]
    all_to_all x1, blocking collectives: 14.5 us -> 9.84 us  [local(): lax.all_to_all(iterate, chips, 0, 0, axis_index_groups=first_groups)]
    ppermute x1, starting transfers between devices: 5.45 us -> 3.51 us  [local(): other = lax.ppermute(mine, 'core', [(0, 1), (1, 0)])]
where the time goes in v9:
time: 89.7 us; the launch traced here: 89.4 us
  blocking collectives  74.2 us (83%)
  Pallas kernels  8.83 us (10%)
  starting transfers between devices  3.51 us (4%)
  waiting for transfers between devices  1.16 us (1%)
  other arithmetic  1.01 us (1%)
    all_to_all x1, blocking collectives, local(): lax.all_to_all(sums.reshape(-1, 1, 128), ('x', 'group'), 0, 0)  24.4 us
    all_to_all x1, blocking collectives, local(): mine = lax.all_to_all(turned, chips, 0, 0, axis_index_groups=second_groups)  20 us
    all_to_all x1, blocking collectives, local(): lax.all_to_all(sums.reshape(-1, 1, 128), ('y', 'core'), 0, 0)  20 us
    all_to_all x1, blocking collectives, local(): lax.all_to_all(iterate, chips, 0, 0, axis_index_groups=first_groups)  9.84 us
    pallas_call x1, Pallas kernels, local(): kernel(functools.partial(iterate_kernel, update_scale), 'newton', shape(g...  5.97 us
    ppermute x1, starting transfers between devices, local(): other = lax.ppermute(mine, 'core', [(0, 1), (1, 0)])  3.51 us
  transfers between devices with their start and end apart: 1, of which 1 were waited for; matrix products, arithmetic and copies ran while one was open for 0% of the time, Pallas kernels for 1%

profile of v9, /device:TPU:1, one launch (start us, length us, event | category | flops | bytes accessed | tf_op | source)
XLA Modules:
  0.0 89.4 jit_solution(1234352232308768521)
XLA Ops:
  0.7 1.0 %broadcast_select_fusion.pair_ref = f32[2,144,128]{2,1,0:T(8,128)S(1)} fusion(f32[144,128]{1,0:T(8,128)} %bitcast.15, f32[144,128]{1,0:T(8,128)} %bitcast.16, pred[2]{0:T(512)(128)(4,1)S(1)} %iota_compare_fusion), kind=kLoop, calls=%fused_computation | loop fusion | flops 36864 | bytes 294914 | tf_op jit(solution)/shard_map/jit(_where)/select_n | solution.py:282
  1.7 0.7 sums.1
  2.3 20.0 %all_to_all.20 = f32[16,1,128]{2,1,0:T(1,128)S(1)} all-to-all(f32[16,1,128]{2,1,0:T(1,128)S(1)} %bitcast.13), channel_id=1, replica_groups=mesh['x'=4,'y'=8,'core'=2,'group'=12] {'y','core'}, dimensions={0} | all-to-all | bytes 16384 | tf_op jit(solution)/shard_map/all_to_all | solution.py:284
  22.3 0.2 combine.1
  22.4 24.4 %all_to_all.21 = f32[48,1,128]{2,1,0:T(1,128)S(1)} all-to-all(f32[48,1,128]{2,1,0:T(1,128)S(1)} %bitcast.11), channel_id=1, replica_groups=mesh['x'=4,'y'=8,'core'=2,'group'=12] {'x','group'}, dimensions={0} | all-to-all | bytes 49152 | tf_op jit(solution)/shard_map/all_to_all | solution.py:286
  46.8 0.2 scale.1
  47.1 9.8 %all_to_all.22.in_ref = bf16[4,144,128]{2,1,0:T(8,128)(2,1)S(1)} all-to-all(bf16[4,144,128]{2,1,0:T(8,128)(2,1)S(1)} %get-tuple-element.13), channel_id=1, replica_groups={{0,48,96,144},{24,72,120,168},{192,240,288,336},{216,264,312,360},{384,..., dimensions={0} | all-to-all | bytes 294912 | tf_op jit(solution)/shard_map/all_to_all | solution.py:293
  56.9 0.5 turn.1
  57.4 20.0 %all_to_all.23.mine_ref = bf16[8,576,128]{2,1,0:T(8,128)(2,1)S(1)} all-to-all(bf16[8,576,128]{2,1,0:T(8,128)(2,1)S(1)} %turn.1), channel_id=1, replica_groups={{0,24,192,216,384,408,576,600},{48,72,240,264,432,456,624,648},{96,120,..., dimensions={0} | all-to-all | bytes 2359296 | tf_op jit(solution)/shard_map/all_to_all | solution.py:301
  77.4 3.5 %collective-permute-start = (bf16[8,576,128]{2,1,0:T(8,128)(2,1)S(1)}, bf16[8,576,128]{2,1,0:T(8,128)(2,1)S(1)}, u32[]{:S(2)}, u32[]{:S(2)}) collective-permute-start(bf16[8,576,128]{2,1,0:T(8,128)(2,1)S(1)} %all_to_all.23.mine_ref), channel_id=1, source_target_pairs={{0,12},{12,0},{1,13},{13,1},{2,14},{14,2},{3,15},{15,3},{4,16},{16... | collective-permute-start | bytes 3538952 | tf_op jit(solution)/shard_map/ppermute | solution.py:302
  81.0 1.3 %gram.1 = (f32[576,576]{1,0:T(8,128)S(1)}, f32[1,144,128]{2,1,0:T(8,128)}) custom-call(bf16[8,576,128]{2,1,0:T(8,128)(2,1)S(1)} %all_to_all.23.mine_ref, f32[2,144,128]{2,1,0:T(8,128)S(1)} %broadcast_select_fusion.pair_ref, f32[8,128]{1,0:T(8,128)S(1)} %get-tuple-element.14.scale_ref), custom_call_target="tpu_custom_call" | custom-call | flops 679477248 | bytes 1179648 | tf_op jit(solution)/shard_map/gram/pallas_call | solution.py:303
  82.2 1.2 %collective-permute-done.other_ref = bf16[8,576,128]{2,1,0:T(8,128)(2,1)S(1)} collective-permute-done((bf16[8,576,128]{2,1,0:T(8,128)(2,1)S(1)}, bf16[8,576,128]{2,1,0:T(8,128)(2,1)S(1)}, u32[]{:S(2)}, u32[]{:S(2)}) %collective-permute-start) | collective-permute-done | bytes 1179680 | tf_op jit(solution)/shard_map/ppermute | solution.py:302
  83.4 6.0 %newton.1 = bf16[1,144,128]{2,1,0:T(8,128)(2,1)} custom-call(bf16[8,576,128]{2,1,0:T(8,128)(2,1)S(1)} %all_to_all.23.mine_ref, bf16[8,576,128]{2,1,0:T(8,128)(2,1)S(1)} %collective-permute-done.other_ref, f32[576,576]{1,0:T(8,128)S(1)} %get-tuple-element.16.gram_ref, f32[144,128]{1,0:T(8,128)S(1)} %get-tuple-element.17.own_ref), custom_call_target="tpu_custom_call" | custom-call | tf_op jit(solution)/shard_map/newton/pallas_call | solution.py:310
  (1 shorter events, 0.0 us)
Async XLA Ops:
  77.4 6.0 %collective-permute-start = (bf16[8,576,128]{2,1,0:T(8,128)(2,1)S(1)}, bf16[8,576,128]{2,1,0:T(8,128)(2,1)S(1)}, u32[]{:S(2)}, u32[]{:S(2)}) collective-permute-start(bf16[8,576,128]{2,1,0:T(8,128)(2,1)S(1)} %all_to_all.23.mine_ref), channel_id=1, source_target_pairs={{0,12},{12,0},{1,13},{13,1},{2,14},{14,2},{3,15},{15,3},{4,16},{16... | collective-permute-start | bytes 3538952 | tf_op jit(solution)/shard_map/ppermute | solution.py:302

commit v10 on v9

--- a/solution.py
+++ b/solution.py
@@ -155,16 +155,15 @@
     for i in range(blocks):
         flat_ref[i * rows : (i + 1) * rows, :] = in_ref[i].astype(f32)
     half = blocks * rows // 9
-    for j in range(9):
-        turned = flat_ref[pl.ds(j, half, stride=9), :].T.astype(bf16)
+    low = lax.broadcasted_iota(jnp.int32, (half, 128), 1) < 64
+    flat = [flat_ref[pl.ds(j, half, stride=9), :] for j in range(9)]
+    turned = [pltpu.roll(flat[j], 64, 1) for j in range(4, 9)]
+    for j in range(5):
+        odd = jnp.where(low, turned[j], turned[j + 1]) if j < 4 else turned[4]
+        block = jnp.concatenate([flat[j], odd], 0).T.astype(bf16)
+        width = min(128, ROWS - 128 * j)
         for i in range(copies):
-            if j < 4:
-                out_ref[i, 128 * j : 128 * j + 128, 0:half] = turned
-            elif j == 4:
-                out_ref[i, 512:576, 0:half] = turned[0:64]
-                out_ref[i, 0:64, half : 2 * half] = turned[64:128]
-            else:
-                out_ref[i, 128 * j - 576 : 128 * j - 448, half : 2 * half] = turned
+            out_ref[i, 128 * j : 128 * j + width, :] = block[:width]
 
 
 def own_load(flat_ref, pairs):
@@ -251,7 +250,7 @@
     for core in range(nc):
         for x in range(nx):
             first += [[at(x, y, core) for y in range(parity, ny, 2)] for parity in range(2)]
-        second += [[at(x, y, core) for x in range(nx) for y in ys] for ys in pairings(ny, core)]
+        second += [[at(x, y, core) for x in range(nx) for y in ys] for ys in pairings(ny, 0)]
     return first, second
 
 

time: 89.7 us -> 88.4 us (0.986)
  blocking collectives: 74.2 us -> 70.1 us
  starting transfers between devices: 3.51 us -> 6.55 us
    all_to_all x1, blocking collectives: 20 us -> 15.9 us  [local(): mine = lax.all_to_all(turned, chips, 0, 0, axis_index_groups=second_groups)]
    ppermute x1, starting transfers between devices: 3.51 us -> 6.55 us  [local(): other = lax.ppermute(mine, 'core', [(0, 1), (1, 0)])]
where the time goes in v10:
time: 88.4 us; the launch traced here: 88.1 us
  blocking collectives  70.1 us (79%)
  Pallas kernels  8.58 us (10%)
  starting transfers between devices  6.55 us (7%)
  waiting for transfers between devices  1.17 us (1%)
  other arithmetic  1.01 us (1%)
    all_to_all x1, blocking collectives, local(): lax.all_to_all(sums.reshape(-1, 1, 128), ('x', 'group'), 0, 0)  24.4 us
    all_to_all x1, blocking collectives, local(): lax.all_to_all(sums.reshape(-1, 1, 128), ('y', 'core'), 0, 0)  20 us
    all_to_all x1, blocking collectives, local(): mine = lax.all_to_all(turned, chips, 0, 0, axis_index_groups=second_groups)  15.9 us
    all_to_all x1, blocking collectives, local(): lax.all_to_all(iterate, chips, 0, 0, axis_index_groups=first_groups)  9.84 us
    ppermute x1, starting transfers between devices, local(): other = lax.ppermute(mine, 'core', [(0, 1), (1, 0)])  6.55 us
    pallas_call x1, Pallas kernels, local(): kernel(functools.partial(iterate_kernel, update_scale), 'newton', shape(g...  5.97 us
  transfers between devices with their start and end apart: 1, of which 1 were waited for; matrix products, arithmetic and copies ran while one was open for 0% of the time, Pallas kernels for 1%

profile of v10, /device:TPU:1, one launch (start us, length us, event | category | flops | bytes accessed | tf_op | source)
XLA Modules:
  0.0 88.1 jit_solution(18300838424356205015)
XLA Ops:
  0.7 1.0 %broadcast_select_fusion.pair_ref = f32[2,144,128]{2,1,0:T(8,128)S(1)} fusion(f32[144,128]{1,0:T(8,128)} %bitcast.15, f32[144,128]{1,0:T(8,128)} %bitcast.16, pred[2]{0:T(512)(128)(4,1)S(1)} %iota_compare_fusion), kind=kLoop, calls=%fused_computation | loop fusion | flops 36864 | bytes 294914 | tf_op jit(solution)/shard_map/jit(_where)/select_n | solution.py:281
  1.7 0.7 sums.1
  2.3 20.0 %all_to_all.20 = f32[16,1,128]{2,1,0:T(1,128)S(1)} all-to-all(f32[16,1,128]{2,1,0:T(1,128)S(1)} %bitcast.13), channel_id=1, replica_groups=mesh['x'=4,'y'=8,'core'=2,'group'=12] {'y','core'}, dimensions={0} | all-to-all | bytes 16384 | tf_op jit(solution)/shard_map/all_to_all | solution.py:283
  22.3 0.2 combine.1
  22.4 24.4 %all_to_all.21 = f32[48,1,128]{2,1,0:T(1,128)S(1)} all-to-all(f32[48,1,128]{2,1,0:T(1,128)S(1)} %bitcast.11), channel_id=1, replica_groups=mesh['x'=4,'y'=8,'core'=2,'group'=12] {'x','group'}, dimensions={0} | all-to-all | bytes 49152 | tf_op jit(solution)/shard_map/all_to_all | solution.py:285
  46.8 0.2 scale.1
  47.1 9.8 %all_to_all.22.in_ref = bf16[4,144,128]{2,1,0:T(8,128)(2,1)S(1)} all-to-all(bf16[4,144,128]{2,1,0:T(8,128)(2,1)S(1)} %get-tuple-element.13), channel_id=1, replica_groups={{0,48,96,144},{24,72,120,168},{192,240,288,336},{216,264,312,360},{384,..., dimensions={0} | all-to-all | bytes 294912 | tf_op jit(solution)/shard_map/all_to_all | solution.py:292
  56.9 0.3 turn.1
  57.2 15.9 %all_to_all.23.mine_ref = bf16[8,576,128]{2,1,0:T(8,128)(2,1)S(1)} all-to-all(bf16[8,576,128]{2,1,0:T(8,128)(2,1)S(1)} %turn.1), channel_id=1, replica_groups={{0,24,192,216,384,408,576,600},{48,72,240,264,432,456,624,648},{96,120,..., dimensions={0} | all-to-all | bytes 2359296 | tf_op jit(solution)/shard_map/all_to_all | solution.py:300
  73.1 6.6 %collective-permute-start = (bf16[8,576,128]{2,1,0:T(8,128)(2,1)S(1)}, bf16[8,576,128]{2,1,0:T(8,128)(2,1)S(1)}, u32[]{:S(2)}, u32[]{:S(2)}) collective-permute-start(bf16[8,576,128]{2,1,0:T(8,128)(2,1)S(1)} %all_to_all.23.mine_ref), channel_id=1, source_target_pairs={{0,12},{12,0},{1,13},{13,1},{2,14},{14,2},{3,15},{15,3},{4,16},{16... | collective-permute-start | bytes 3538952 | tf_op jit(solution)/shard_map/ppermute | solution.py:301
  79.7 1.3 %gram.1 = (f32[576,576]{1,0:T(8,128)S(1)}, f32[1,144,128]{2,1,0:T(8,128)}) custom-call(bf16[8,576,128]{2,1,0:T(8,128)(2,1)S(1)} %all_to_all.23.mine_ref, f32[2,144,128]{2,1,0:T(8,128)S(1)} %broadcast_select_fusion.pair_ref, f32[8,128]{1,0:T(8,128)S(1)} %get-tuple-element.14.scale_ref), custom_call_target="tpu_custom_call" | custom-call | flops 679477248 | bytes 1179648 | tf_op jit(solution)/shard_map/gram/pallas_call | solution.py:302
  81.0 1.2 %collective-permute-done.other_ref = bf16[8,576,128]{2,1,0:T(8,128)(2,1)S(1)} collective-permute-done((bf16[8,576,128]{2,1,0:T(8,128)(2,1)S(1)}, bf16[8,576,128]{2,1,0:T(8,128)(2,1)S(1)}, u32[]{:S(2)}, u32[]{:S(2)}) %collective-permute-start) | collective-permute-done | bytes 1179680 | tf_op jit(solution)/shard_map/ppermute | solution.py:301
  82.1 6.0 %newton.1 = bf16[1,144,128]{2,1,0:T(8,128)(2,1)} custom-call(bf16[8,576,128]{2,1,0:T(8,128)(2,1)S(1)} %all_to_all.23.mine_ref, bf16[8,576,128]{2,1,0:T(8,128)(2,1)S(1)} %collective-permute-done.other_ref, f32[576,576]{1,0:T(8,128)S(1)} %get-tuple-element.16.gram_ref, f32[144,128]{1,0:T(8,128)S(1)} %get-tuple-element.17.own_ref), custom_call_target="tpu_custom_call" | custom-call | tf_op jit(solution)/shard_map/newton/pallas_call | solution.py:309
  (1 shorter events, 0.0 us)
Async XLA Ops:
  73.1 9.0 %collective-permute-start = (bf16[8,576,128]{2,1,0:T(8,128)(2,1)S(1)}, bf16[8,576,128]{2,1,0:T(8,128)(2,1)S(1)}, u32[]{:S(2)}, u32[]{:S(2)}) collective-permute-start(bf16[8,576,128]{2,1,0:T(8,128)(2,1)S(1)} %all_to_all.23.mine_ref), channel_id=1, source_target_pairs={{0,12},{12,0},{1,13},{13,1},{2,14},{14,2},{3,15},{15,3},{4,16},{16... | collective-permute-start | bytes 3538952 | tf_op jit(solution)/shard_map/ppermute | solution.py:301

commit v11 on v10

--- a/solution.py
+++ b/solution.py
@@ -250,7 +250,7 @@
     for core in range(nc):
         for x in range(nx):
             first += [[at(x, y, core) for y in range(parity, ny, 2)] for parity in range(2)]
-        second += [[at(x, y, core) for x in range(nx) for y in ys] for ys in pairings(ny, 0)]
+        second += [[at(x, y, core) for y in ys for x in range(nx)] for ys in pairings(ny, 0)]
     return first, second
 
 

time: 88.4 us -> 88.3 us (level)
  no operation moved by 1% of the time
where the time goes in v11:
time: 88.3 us; the launch traced here: 88 us
  blocking collectives  69.8 us (79%)
  Pallas kernels  8.58 us (10%)
  starting transfers between devices  6.84 us (8%)
  waiting for transfers between devices  1.16 us (1%)
  other arithmetic  1.01 us (1%)
    all_to_all x1, blocking collectives, local(): lax.all_to_all(sums.reshape(-1, 1, 128), ('x', 'group'), 0, 0)  24.4 us
    all_to_all x1, blocking collectives, local(): lax.all_to_all(sums.reshape(-1, 1, 128), ('y', 'core'), 0, 0)  20 us
    all_to_all x1, blocking collectives, local(): mine = lax.all_to_all(turned, chips, 0, 0, axis_index_groups=second_groups)  15.6 us
    all_to_all x1, blocking collectives, local(): lax.all_to_all(iterate, chips, 0, 0, axis_index_groups=first_groups)  9.84 us
    ppermute x1, starting transfers between devices, local(): other = lax.ppermute(mine, 'core', [(0, 1), (1, 0)])  6.84 us
    pallas_call x1, Pallas kernels, local(): kernel(functools.partial(iterate_kernel, update_scale), 'newton', shape(g...  5.97 us
  transfers between devices with their start and end apart: 1, of which 1 were waited for; matrix products, arithmetic and copies ran while one was open for 0% of the time, Pallas kernels for 1%

profile of v11, /device:TPU:1, one launch (start us, length us, event | category | flops | bytes accessed | tf_op | source)
XLA Modules:
  0.0 88.0 jit_solution(10874352874745379550)
XLA Ops:
  0.7 1.0 %broadcast_select_fusion.pair_ref = f32[2,144,128]{2,1,0:T(8,128)S(1)} fusion(f32[144,128]{1,0:T(8,128)} %bitcast.15, f32[144,128]{1,0:T(8,128)} %bitcast.16, pred[2]{0:T(512)(128)(4,1)S(1)} %iota_compare_fusion), kind=kLoop, calls=%fused_computation | loop fusion | flops 36864 | bytes 294914 | tf_op jit(solution)/shard_map/jit(_where)/select_n | solution.py:281
  1.7 0.7 sums.1
  2.3 20.0 %all_to_all.20 = f32[16,1,128]{2,1,0:T(1,128)S(1)} all-to-all(f32[16,1,128]{2,1,0:T(1,128)S(1)} %bitcast.13), channel_id=1, replica_groups=mesh['x'=4,'y'=8,'core'=2,'group'=12] {'y','core'}, dimensions={0} | all-to-all | bytes 16384 | tf_op jit(solution)/shard_map/all_to_all | solution.py:283
  22.3 0.2 combine.1
  22.4 24.4 %all_to_all.21 = f32[48,1,128]{2,1,0:T(1,128)S(1)} all-to-all(f32[48,1,128]{2,1,0:T(1,128)S(1)} %bitcast.11), channel_id=1, replica_groups=mesh['x'=4,'y'=8,'core'=2,'group'=12] {'x','group'}, dimensions={0} | all-to-all | bytes 49152 | tf_op jit(solution)/shard_map/all_to_all | solution.py:285
  46.8 0.2 scale.1
  47.1 9.8 %all_to_all.22.in_ref = bf16[4,144,128]{2,1,0:T(8,128)(2,1)S(1)} all-to-all(bf16[4,144,128]{2,1,0:T(8,128)(2,1)S(1)} %get-tuple-element.13), channel_id=1, replica_groups={{0,48,96,144},{24,72,120,168},{192,240,288,336},{216,264,312,360},{384,..., dimensions={0} | all-to-all | bytes 294912 | tf_op jit(solution)/shard_map/all_to_all | solution.py:292
  56.9 0.3 turn.1
  57.2 15.6 %all_to_all.23.mine_ref = bf16[8,576,128]{2,1,0:T(8,128)(2,1)S(1)} all-to-all(bf16[8,576,128]{2,1,0:T(8,128)(2,1)S(1)} %turn.1), channel_id=1, replica_groups={{0,192,384,576,24,216,408,600},{48,240,432,624,72,264,456,648},{96,288,..., dimensions={0} | all-to-all | bytes 2359296 | tf_op jit(solution)/shard_map/all_to_all | solution.py:300
  72.8 6.8 %collective-permute-start = (bf16[8,576,128]{2,1,0:T(8,128)(2,1)S(1)}, bf16[8,576,128]{2,1,0:T(8,128)(2,1)S(1)}, u32[]{:S(2)}, u32[]{:S(2)}) collective-permute-start(bf16[8,576,128]{2,1,0:T(8,128)(2,1)S(1)} %all_to_all.23.mine_ref), channel_id=1, source_target_pairs={{0,12},{12,0},{1,13},{13,1},{2,14},{14,2},{3,15},{15,3},{4,16},{16... | collective-permute-start | bytes 3538952 | tf_op jit(solution)/shard_map/ppermute | solution.py:301
  79.6 1.3 %gram.1 = (f32[576,576]{1,0:T(8,128)S(1)}, f32[1,144,128]{2,1,0:T(8,128)}) custom-call(bf16[8,576,128]{2,1,0:T(8,128)(2,1)S(1)} %all_to_all.23.mine_ref, f32[2,144,128]{2,1,0:T(8,128)S(1)} %broadcast_select_fusion.pair_ref, f32[8,128]{1,0:T(8,128)S(1)} %get-tuple-element.14.scale_ref), custom_call_target="tpu_custom_call" | custom-call | flops 679477248 | bytes 1179648 | tf_op jit(solution)/shard_map/gram/pallas_call | solution.py:302
  80.9 1.2 %collective-permute-done.other_ref = bf16[8,576,128]{2,1,0:T(8,128)(2,1)S(1)} collective-permute-done((bf16[8,576,128]{2,1,0:T(8,128)(2,1)S(1)}, bf16[8,576,128]{2,1,0:T(8,128)(2,1)S(1)}, u32[]{:S(2)}, u32[]{:S(2)}) %collective-permute-start) | collective-permute-done | bytes 1179680 | tf_op jit(solution)/shard_map/ppermute | solution.py:301
  82.1 6.0 %newton.1 = bf16[1,144,128]{2,1,0:T(8,128)(2,1)} custom-call(bf16[8,576,128]{2,1,0:T(8,128)(2,1)S(1)} %all_to_all.23.mine_ref, bf16[8,576,128]{2,1,0:T(8,128)(2,1)S(1)} %collective-permute-done.other_ref, f32[576,576]{1,0:T(8,128)S(1)} %get-tuple-element.16.gram_ref, f32[144,128]{1,0:T(8,128)S(1)} %get-tuple-element.17.own_ref), custom_call_target="tpu_custom_call" | custom-call | tf_op jit(solution)/shard_map/newton/pallas_call | solution.py:309
  (1 shorter events, 0.0 us)
Async XLA Ops:
  72.8 9.3 %collective-permute-start = (bf16[8,576,128]{2,1,0:T(8,128)(2,1)S(1)}, bf16[8,576,128]{2,1,0:T(8,128)(2,1)S(1)}, u32[]{:S(2)}, u32[]{:S(2)}) collective-permute-start(bf16[8,576,128]{2,1,0:T(8,128)(2,1)S(1)} %all_to_all.23.mine_ref), channel_id=1, source_target_pairs={{0,12},{12,0},{1,13},{13,1},{2,14},{14,2},{3,15},{15,3},{4,16},{16... | collective-permute-start | bytes 3538952 | tf_op jit(solution)/shard_map/ppermute | solution.py:301

commit v12 on v10

--- a/solution.py
+++ b/solution.py
@@ -99,7 +99,7 @@
     return fast_two_sum(high, low + pltpu.roll(high, 64, 1))
 
 
-def sums_kernel(pair_ref, out_ref):
+def sums_kernel(groups, group_ref, pair_ref, out_ref):
     gg, gm, mm = [], [], []
     for i in range(0, pair_ref.shape[1], 8):
         g = pair_ref[0, i : i + 8, :]
@@ -110,17 +110,16 @@
     sums = [fold(fold(tree(v), 0, (4, 2, 1)), 1, (64, 32, 16, 8, 4, 2, 1)) for v in (gg, gm, mm)]
     tile = pack([fast_two_sum(*v) for v in [sums[0]] + sums])
     for i in range(0, out_ref.shape[0], 8):
+        to = lax.rem(lax.broadcasted_iota(jnp.int32, (8, 128), 0) + i, groups)
+        keep = (to == group_ref[0]) | (lax.rem(lanes(), 64) == 0)
+        out_ref[i : i + 8, :] = jnp.where(keep, tile, 0.0)
+
+
+def combine_kernel(in_ref, out_ref):
+    high, low = add_rows(in_ref)
+    tile = jnp.where(lanes() < 64, high, pltpu.roll(low, 64, 1))
+    for i in range(0, out_ref.shape[0], 8):
         out_ref[i : i + 8, :] = tile
-
-
-def combine_kernel(groups, group_ref, in_ref, out_ref):
-    high, low = add_rows(in_ref)
-    lane = lanes()
-    tile = jnp.where(lane < 64, high, pltpu.roll(low, 64, 1))
-    for i in range(0, out_ref.shape[0], 8):
-        to = lax.rem(lax.broadcasted_iota(jnp.int32, (8, 128), 0) + i, groups)
-        keep = (to == group_ref[0]) | (lax.rem(lane, 64) == 0)
-        out_ref[i : i + 8, :] = jnp.where(keep, tile, 0.0)
 
 
 def scale_kernel(entries, in_ref, pair_ref, out_ref, own_ref, scale_ref):
@@ -279,10 +278,10 @@
     grad, momentum, group = lax.optimization_barrier((grad, momentum, group))
     first = lax.broadcasted_iota(jnp.int32, (2, rows, 128), 0) == 0
     pair = jnp.where(first, grad, momentum)
-    sums = kernel(sums_kernel, "sums", shape((ny * nc, 128), f32), [VMEM])(pair)
+    sums = kernel(functools.partial(sums_kernel, ng), "sums", shape((nx * ng, 128), f32), [SMEM, VMEM])(group, pair)
+    sums = lax.all_to_all(sums.reshape(-1, 1, 128), ("x", "group"), 0, 0).reshape(-1, 128)
+    sums = kernel(combine_kernel, "combine", shape((ny * nc, 128), f32), [VMEM])(sums)
     sums = lax.all_to_all(sums.reshape(-1, 1, 128), ("y", "core"), 0, 0).reshape(-1, 128)
-    sums = kernel(functools.partial(combine_kernel, ng), "combine", shape((nx * ng, 128), f32), [SMEM, VMEM])(group, sums)
-    sums = lax.all_to_all(sums.reshape(-1, 1, 128), ("x", "group"), 0, 0).reshape(-1, 128)
     iterate, own, scale = kernel(
         functools.partial(scale_kernel, entries),
         "scale",

time: 88.4 us -> 89.9 us (1.017)
  blocking collectives: 70.1 us -> 72.2 us
    all_to_all x1, blocking collectives: 24.4 us -> 29.8 us  [local(): lax.all_to_all(sums.reshape(-1, 1, 128), ('x', 'group'), 0, 0)]
    all_to_all x1, blocking collectives: 20 us -> 16 us  [local(): lax.all_to_all(sums.reshape(-1, 1, 128), ('y', 'core'), 0, 0)]
where the time goes in v12:
time: 89.9 us; the launch traced here: 89.6 us
  blocking collectives  72.2 us (80%)
  Pallas kernels  8.58 us (10%)
  starting transfers between devices  5.98 us (7%)
  waiting for transfers between devices  1.17 us (1%)
  other arithmetic  1.01 us (1%)
    all_to_all x1, blocking collectives, local(): lax.all_to_all(sums.reshape(-1, 1, 128), ('x', 'group'), 0, 0)  29.8 us
    all_to_all x1, blocking collectives, local(): mine = lax.all_to_all(turned, chips, 0, 0, axis_index_groups=second_groups)  16.5 us
    all_to_all x1, blocking collectives, local(): lax.all_to_all(sums.reshape(-1, 1, 128), ('y', 'core'), 0, 0)  16 us
    all_to_all x1, blocking collectives, local(): lax.all_to_all(iterate, chips, 0, 0, axis_index_groups=first_groups)  9.88 us
    ppermute x1, starting transfers between devices, local(): other = lax.ppermute(mine, 'core', [(0, 1), (1, 0)])  5.98 us
    pallas_call x1, Pallas kernels, local(): kernel(functools.partial(iterate_kernel, update_scale), 'newton', shape(g...  5.97 us
  transfers between devices with their start and end apart: 1, of which 1 were waited for; matrix products, arithmetic and copies ran while one was open for 0% of the time, Pallas kernels for 1%

profile of v12, /device:TPU:1, one launch (start us, length us, event | category | flops | bytes accessed | tf_op | source)
XLA Modules:
  0.0 89.6 jit_solution(10959559413860101735)
XLA Ops:
  0.7 1.0 %broadcast_select_fusion.pair_ref = f32[2,144,128]{2,1,0:T(8,128)S(1)} fusion(f32[144,128]{1,0:T(8,128)} %bitcast.15, f32[144,128]{1,0:T(8,128)} %bitcast.16, pred[2]{0:T(512)(128)(4,1)S(1)} %iota_compare_fusion), kind=kLoop, calls=%fused_computation | loop fusion | flops 36864 | bytes 294914 | tf_op jit(solution)/shard_map/jit(_where)/select_n | solution.py:280
  1.7 0.7 sums.1
  2.3 29.8 %all_to_all.20 = f32[48,1,128]{2,1,0:T(1,128)S(1)} all-to-all(f32[48,1,128]{2,1,0:T(1,128)S(1)} %bitcast.12), channel_id=1, replica_groups=mesh['x'=4,'y'=8,'core'=2,'group'=12] {'x','group'}, dimensions={0} | all-to-all | bytes 49152 | tf_op jit(solution)/shard_map/all_to_all | solution.py:282
  32.1 0.2 combine.1
  32.2 16.0 %all_to_all.21 = f32[16,1,128]{2,1,0:T(1,128)S(1)} all-to-all(f32[16,1,128]{2,1,0:T(1,128)S(1)} %bitcast.14), channel_id=1, replica_groups=mesh['x'=4,'y'=8,'core'=2,'group'=12] {'y','core'}, dimensions={0} | all-to-all | bytes 16384 | tf_op jit(solution)/shard_map/all_to_all | solution.py:284
  48.2 0.2 scale.1
  48.5 9.9 %all_to_all.22.in_ref = bf16[4,144,128]{2,1,0:T(8,128)(2,1)S(1)} all-to-all(bf16[4,144,128]{2,1,0:T(8,128)(2,1)S(1)} %get-tuple-element.13), channel_id=1, replica_groups={{0,48,96,144},{24,72,120,168},{192,240,288,336},{216,264,312,360},{384,..., dimensions={0} | all-to-all | bytes 294912 | tf_op jit(solution)/shard_map/all_to_all | solution.py:291
  58.4 0.3 turn.1
  58.7 16.5 %all_to_all.23.mine_ref = bf16[8,576,128]{2,1,0:T(8,128)(2,1)S(1)} all-to-all(bf16[8,576,128]{2,1,0:T(8,128)(2,1)S(1)} %turn.1), channel_id=1, replica_groups={{0,24,192,216,384,408,576,600},{48,72,240,264,432,456,624,648},{96,120,..., dimensions={0} | all-to-all | bytes 2359296 | tf_op jit(solution)/shard_map/all_to_all | solution.py:299
  75.2 6.0 %collective-permute-start = (bf16[8,576,128]{2,1,0:T(8,128)(2,1)S(1)}, bf16[8,576,128]{2,1,0:T(8,128)(2,1)S(1)}, u32[]{:S(2)}, u32[]{:S(2)}) collective-permute-start(bf16[8,576,128]{2,1,0:T(8,128)(2,1)S(1)} %all_to_all.23.mine_ref), channel_id=1, source_target_pairs={{0,12},{12,0},{1,13},{13,1},{2,14},{14,2},{3,15},{15,3},{4,16},{16... | collective-permute-start | bytes 3538952 | tf_op jit(solution)/shard_map/ppermute | solution.py:300
  81.1 1.3 %gram.1 = (f32[576,576]{1,0:T(8,128)S(1)}, f32[1,144,128]{2,1,0:T(8,128)}) custom-call(bf16[8,576,128]{2,1,0:T(8,128)(2,1)S(1)} %all_to_all.23.mine_ref, f32[2,144,128]{2,1,0:T(8,128)S(1)} %broadcast_select_fusion.pair_ref, f32[8,128]{1,0:T(8,128)S(1)} %get-tuple-element.14.scale_ref), custom_call_target="tpu_custom_call" | custom-call | flops 679477248 | bytes 1179648 | tf_op jit(solution)/shard_map/gram/pallas_call | solution.py:301
  82.4 1.2 %collective-permute-done.other_ref = bf16[8,576,128]{2,1,0:T(8,128)(2,1)S(1)} collective-permute-done((bf16[8,576,128]{2,1,0:T(8,128)(2,1)S(1)}, bf16[8,576,128]{2,1,0:T(8,128)(2,1)S(1)}, u32[]{:S(2)}, u32[]{:S(2)}) %collective-permute-start) | collective-permute-done | bytes 1179680 | tf_op jit(solution)/shard_map/ppermute | solution.py:300
  83.6 6.0 %newton.1 = bf16[1,144,128]{2,1,0:T(8,128)(2,1)} custom-call(bf16[8,576,128]{2,1,0:T(8,128)(2,1)S(1)} %all_to_all.23.mine_ref, bf16[8,576,128]{2,1,0:T(8,128)(2,1)S(1)} %collective-permute-done.other_ref, f32[576,576]{1,0:T(8,128)S(1)} %get-tuple-element.16.gram_ref, f32[144,128]{1,0:T(8,128)S(1)} %get-tuple-element.17.own_ref), custom_call_target="tpu_custom_call" | custom-call | tf_op jit(solution)/shard_map/newton/pallas_call | solution.py:308
  (1 shorter events, 0.0 us)
Async XLA Ops:
  75.2 8.4 %collective-permute-start = (bf16[8,576,128]{2,1,0:T(8,128)(2,1)S(1)}, bf16[8,576,128]{2,1,0:T(8,128)(2,1)S(1)}, u32[]{:S(2)}, u32[]{:S(2)}) collective-permute-start(bf16[8,576,128]{2,1,0:T(8,128)(2,1)S(1)} %all_to_all.23.mine_ref), channel_id=1, source_target_pairs={{0,12},{12,0},{1,13},{13,1},{2,14},{14,2},{3,15},{15,3},{4,16},{16... | collective-permute-start | bytes 3538952 | tf_op jit(solution)/shard_map/ppermute | solution.py:300
